TPU v7x, 512 devices: a whole 4x4x16 slice. The times are simulated.
512 devices in a mesh: band: 16 (over z), region: 32 (over y, x, core).
Axes of the slice: x: 4, y: 4, z: 16, core: 2. Of those that a mesh axis runs over, the one named last changes fastest.
Arguments:
- values: float32 [131072, 128], P(('band', 'region')), may hold values from -9 to 9
- coords: float32 [2, 131072], P(None, ('band', 'region')), may hold values from 0 to 2
- neighbours: int32 [1024, 256], P(('band', 'region')), may hold values from 0 to 131071, as said below
- log_params: float32 [3], replicated, may hold values from -0.5 to 0.5
Outputs:
- grad_values: float32 [131072, 128], P(('band', 'region'))
- grad_params: float32 [3], replicated
Inputs may be any that keep to these rules, and one draw needn't show every extreme that they name: `neighbours`: the 256 indices of a block are distinct and none lies in the block. 160 of them lie on other devices of the block's band; in band 0 the others lie on the block's own device; in other bands 64 lie on the own device and 32 among the last 64 points of the device of the band below with the same region index. The blocks of one device use at most 11 distinct points of any other device of their band, in at most 22 entries, and both bounds are reached for some device pair of every device.
All inputs are finite; a program needn't handle non-finite values.
Results may differ from a plain program's by a relative error of at most 0.0003.
Values sent between devices are 32-bit elements; how exact they have to be, the bound alone decides.
A program may use at most 64 MiB of HBM per device.

v0:
```python
import jax
import jax.numpy as jnp
from jax import lax
from jax.sharding import PartitionSpec as P

M = 256
RIM = 64
POOL = 160


def passed_along(x, axis, by):
    devices = lax.axis_size(axis)
    pairs = [(i, i + by) for i in range(devices) if 0 <= i + by < devices]
    return lax.ppermute(x, axis, pairs)


def block_grads(joint_rows, joint_coords, params):
    highest = lax.Precision.HIGHEST
    delta_x = joint_coords[:, 0][:, None] - joint_coords[:, 0][None, :]
    delta_y = joint_coords[:, 1][:, None] - joint_coords[:, 1][None, :]
    distance = jnp.sqrt(delta_x * delta_x + delta_y * delta_y)
    variance = jnp.exp(params[0])
    inverse_range = jnp.sqrt(3.0) * jnp.exp(-params[1])
    nugget = jnp.exp(params[2])
    scaled = inverse_range * distance
    decay = jnp.exp(-scaled)
    shape_part = (1.0 + scaled) * decay
    order_n = joint_rows.shape[0]
    reps = joint_rows.shape[1]
    identity = jnp.eye(order_n, dtype=jnp.float32)
    kernel = variance * shape_part + nugget * identity
    factor = jnp.linalg.cholesky(kernel)
    inverse = jax.scipy.linalg.solve_triangular(factor, identity, lower=True)
    tail_inv = inverse[M:]
    tail_z = jnp.dot(tail_inv, joint_rows, precision=highest)
    back = jnp.dot(tail_inv.T, tail_z, precision=highest)
    head_inv = inverse[:M, :M]
    head_z = jnp.dot(head_inv, joint_rows[:M], precision=highest)
    head_a = jnp.dot(head_inv.T, head_z, precision=highest)
    padded = jnp.concatenate([head_a, jnp.zeros((order_n - M, reps), jnp.float32)], axis=0)
    cross = jnp.dot(padded, back.T, precision=highest)
    grad_kernel = 0.5 * (
        cross + cross.T + jnp.dot(back, back.T, precision=highest)
    ) - 0.5 * reps * jnp.dot(tail_inv.T, tail_inv, precision=highest)
    grad_var = jnp.sum(grad_kernel * (variance * shape_part))
    grad_range = jnp.sum(grad_kernel * (variance * scaled * scaled * decay))
    grad_nugget = nugget * jnp.trace(grad_kernel)
    return (-back, jnp.stack([grad_var, grad_range, grad_nugget]))


def shards(values, coords, neighbours, log_params):
    n_reg = lax.axis_size("region")
    n_all = lax.axis_size("band") * n_reg
    band_id = lax.axis_index("band")
    reg_id = lax.axis_index("region")
    points_here = values.shape[0]
    reps = values.shape[1]
    blocks_here = neighbours.shape[0]
    width = neighbours.shape[1]
    block_len = points_here // blocks_here
    my_device = band_id * n_reg + reg_id
    coord_rows = coords.T
    rim_start = points_here - RIM
    rim_rows, rim_coords = passed_along((values[rim_start:], coord_rows[rim_start:]), "band", 1)
    flat_list = neighbours.reshape(-1)
    owner_dev = flat_list // points_here
    offset = flat_list % points_here
    owner_band = owner_dev // n_reg
    owner_reg = owner_dev % n_reg
    is_local = owner_dev == my_device
    is_rim = owner_band == band_id - 1
    is_far = jnp.logical_and(owner_band == band_id, owner_reg != reg_id)
    cap_points = (2 * POOL + n_reg - 2) // (n_reg - 1)
    capacity = 2 * cap_points
    one_hot = jnp.logical_and(
        owner_reg[:, None] == jnp.arange(n_reg)[None, :], is_far[:, None]
    ).astype(jnp.int32)
    before = jnp.cumsum(one_hot, axis=0) - one_hot
    slot_rank = jnp.sum(before * one_hot, axis=1)
    far_slot = owner_reg * capacity + slot_rank
    total_slots = n_reg * capacity
    requests = (
        jnp.zeros((total_slots,), jnp.int32)
        .at[jnp.where(is_far, far_slot, total_slots)]
        .set(offset, mode="drop")
    )
    requests = requests.reshape(n_reg, capacity)
    requested = lax.all_to_all(requests, "region", split_axis=0, concat_axis=0, tiled=True)
    got_rows, got_coords, requested = (
        lax.all_to_all(values[requested], "region", split_axis=0, concat_axis=0, tiled=True),
        lax.all_to_all(coord_rows[requested], "region", split_axis=0, concat_axis=0, tiled=True),
        requested,
    )
    row_table = jnp.concatenate([values, rim_rows, got_rows.reshape(-1, reps)], axis=0)
    coord_table = jnp.concatenate([coord_rows, rim_coords, got_coords.reshape(-1, 2)], axis=0)
    entry_index = jnp.where(
        is_local,
        offset,
        jnp.where(is_rim, points_here + offset - rim_start, points_here + RIM + far_slot),
    )
    near_rows = row_table[entry_index].reshape(blocks_here, width, reps)
    near_coords = coord_table[entry_index].reshape(blocks_here, width, 2)
    joint_rows = jnp.concatenate([near_rows, values.reshape(blocks_here, block_len, reps)], axis=1)
    joint_coords = jnp.concatenate(
        [near_coords, coord_rows.reshape(blocks_here, block_len, 2)], axis=1
    )
    grad_joint, theta_terms = jax.vmap(block_grads, (0, 0, None))(
        joint_rows, joint_coords, log_params
    )
    grad_theta = jnp.sum(theta_terms, axis=0)
    grad_near = grad_joint[:, :width].reshape(-1, reps)
    grad_own = grad_joint[:, width:].reshape(points_here, reps)
    zero_rows = jnp.zeros_like(grad_near)
    local_part = jax.ops.segment_sum(
        jnp.where(is_local[:, None], grad_near, zero_rows),
        jnp.where(is_local, offset, 0),
        points_here,
    )
    rim_part = jax.ops.segment_sum(
        jnp.where(is_rim[:, None], grad_near, zero_rows),
        jnp.where(is_rim, offset - rim_start, 0),
        RIM,
    )
    rim_back = passed_along(rim_part, "band", -1)
    far_terms = jax.ops.segment_sum(
        jnp.where(is_far[:, None], grad_near, zero_rows),
        jnp.where(is_far, far_slot, 0),
        total_slots,
    )
    far_terms = far_terms.reshape(n_reg, capacity, reps)
    returned = lax.all_to_all(far_terms, "region", split_axis=0, concat_axis=0, tiled=True)
    far_part = jax.ops.segment_sum(returned.reshape(-1, reps), requested.reshape(-1), points_here)
    grad_values = (grad_own + local_part + far_part).at[rim_start:].add(rim_back)
    theta_total = lax.psum(grad_theta, ("band", "region"))
    grad_params = theta_total / (points_here * n_all * reps)
    return (grad_values, grad_params)


def solution(mesh):
    placed = (
        P(("band", "region"), None),
        P(None, ("band", "region")),
        P(("band", "region"), None),
        P(),
    )
    return jax.shard_map(
        shards,
        mesh=mesh,
        in_specs=placed,
        out_specs=(P(("band", "region"), None), P()),
        check_vma=False,
    )
```

profile of v0, /device:TPU:1, one launch (start us, length us, event | category | flops | bytes accessed | tf_op | source)
XLA Modules:
  0.0 396.2 jit_solution(124038978400748761)
XLA Ops:
  3.2 1.2 reduce-window.6
  7.3 2.4 scatter_custom_fusion
  10.4 10.4 %all-to-all-start = ((s32[32,1,22]{2,1,0:T(1,128)}), s32[32,1,22]{2,1,0:T(1,128)S(1)}, u32[]{:S(2)}, u32[]{:S(2)}) async-start(s32[32,1,22]{2,1,0:T(1,128)} %bitcast.6), calls=%async_computation | async-start | bytes 32768 | tf_op jit(solution)/shard_map/all_to_all | solution.py:88
  21.6 1.8 collective-permute-start
  23.4 1.4 slice.151
  24.8 4.1 %collective-permute-start.1 = (f32[64,128]{1,0:T(8,128)}, f32[64,128]{1,0:T(8,128)}, u32[]{:S(2)}, u32[]{:S(2)}) collective-permute-start(f32[64,128]{1,0:T(8,128)} %slice.151), channel_id=1, source_target_pairs={{0,32},{32,64},{64,96},{96,128},{128,160},{160,192},{192,224},{224... | collective-permute-start | bytes 98312 | tf_op jit(solution)/shard_map/ppermute | solution.py:14
  33.3 1.7 gather_fusion
  35.9 7.9 %all-to-all-start.1 = ((f32[32,22,2]{1,2,0:T(2,128)}), f32[32,22,2]{1,2,0:T(2,128)S(1)}, u32[]{:S(2)}, u32[]{:S(2)}) async-start(f32[32,22,2]{1,2,0:T(2,128)} %copy.64), calls=%async_computation.1 | async-start | bytes 65536 | tf_op jit(solution)/shard_map/all_to_all | solution.py:91
  45.9 1.7 gather_fusion.2
  49.0 1.3 reduce.26
  51.1 7.3 %all-to-all-start.2 = ((f32[32,22,128]{2,1,0:T(8,128)}), f32[32,22,128]{2,1,0:T(8,128)}, u32[]{:S(2)}, u32[]{:S(2)}) async-start(f32[32,22,128]{2,1,0:T(8,128)} %reshape.576), calls=%async_computation.2 | async-start | bytes 786432 | tf_op jit(solution)/shard_map/all_to_all | solution.py:90
  60.0 1.6 add_multiply_fusion
  61.7 23.5 %custom-call.26 = f32[2,128,128]{2,1,0:T(8,128)S(1)} custom-call(f32[2,128,128]{2,1,0:T(8,128)S(1)} %cholesky.198), custom_call_target="Cholesky" | custom-call | tf_op jit(solution)/shard_map/vmap(jit(cholesky))/cholesky | solution.py:32
  85.2 19.7 %custom-call.27 = f32[2,1,128,128]{2,3,1,0:T(8,128)S(1)} custom-call(f32[2,1,128,128]{3,2,1,0:T(8,128)S(1)} %select_bitcast_fusion.1), custom_call_target="InvertDiagBlocksLowerTriangular" | custom-call | tf_op jit(solution)/shard_map/vmap(jit(cholesky))/cholesky | solution.py:32
  105.7 23.6 %custom-call.28 = f32[2,128,128]{2,1,0:T(8,128)S(1)} custom-call(f32[2,128,128]{2,1,0:T(8,128)S(1)} %cholesky.202), custom_call_target="Cholesky" | custom-call | tf_op jit(solution)/shard_map/vmap(jit(cholesky))/cholesky | solution.py:32
  129.4 20.3 %custom-call.29 = f32[2,1,128,128]{2,3,1,0:T(8,128)} custom-call(f32[2,1,128,128]{3,2,1,0:T(8,128)S(1)} %get-tuple-element.55), custom_call_target="InvertDiagBlocksLowerTriangular" | custom-call | tf_op jit(solution)/shard_map/vmap(jit(cholesky))/cholesky | solution.py:32
  151.2 23.5 %custom-call.30 = f32[2,128,128]{2,1,0:T(8,128)S(1)} custom-call(f32[2,128,128]{2,1,0:T(8,128)S(1)} %convolution_subtract_fusion.3), custom_call_target="Cholesky" | custom-call | tf_op jit(solution)/shard_map/vmap(jit(cholesky))/cholesky | solution.py:32
  175.8 8.3 %while.2 = (s32[]{:T(128)}, f32[2,384,384]{2,1,0:T(8,128)S(1)}, s32[3,2]{0,1:T(2,128)S(1)}, f32[3,2,128,128]{3,2,0,1:T(8,128)}, s32[]{:T(128)}) while((s32[]{:T(128)}, f32[2,384,384]{2,1,0:T(8,128)S(1)}, s32[3,2]{0,1:T(2,128)S(1)}, f32[3,2,128,128]{3,2,0,1:T(8,128)}, s32[]{:T(128)}) %tuple.54), condition=%wide.while_cond.1, body=%wide.while_body.1.sunk | while | flops 2 | bytes 263777 | solution.py:33
  176.5 2.1 bitcast_dynamic-update-slice_fusion.2
  179.3 2.1 bitcast_dynamic-update-slice_fusion.2
  182.0 2.1 bitcast_dynamic-update-slice_fusion.2
  184.1 60.0 %custom-call.31 = f32[2,3,128,128]{2,3,1,0:T(8,128)S(1)} custom-call(f32[2,3,128,128]{3,2,1,0:T(8,128)} %bitcast.20), custom_call_target="InvertDiagBlocksLowerTriangular" | custom-call | tf_op jit(solution)/shard_map/vmap(jit(_solve_triangular))/triangular_solve | solution.py:33
  246.3 1.4 fusion.29
  255.2 2.2 fusion.1
  257.7 2.9 scatter_custom_fusion.2
  261.4 7.4 %all-to-all-start.3 = ((f32[32,22,128]{2,1,0:T(8,128)}), f32[32,22,128]{2,1,0:T(8,128)S(1)}, u32[]{:S(2)}, u32[]{:S(2)}) async-start(f32[32,22,128]{2,1,0:T(8,128)} %reshape.536), calls=%async_computation.3 | async-start | bytes 786432 | tf_op jit(solution)/shard_map/all_to_all | solution.py:131
  268.9 2.3 multiply_reduce_fusion
  271.4 107.7 %psum.7 = f32[3]{0:T(128)S(1)} all-reduce(f32[3]{0:T(128)S(1)} %maximum_reduce_fusion), channel_id=1, replica_groups=mesh['band'=16,'region'=32] {'band','region'}, use_global_device_ids=true, to_apply=%region_18.19 | all-reduce | flops 3 | bytes 24 | tf_op jit(solution)/shard_map/psum | solution.py:134
  379.1 4.2 %scatter_custom_fusion.4 = f32[64,128]{1,0:T(8,128)S(1)} fusion(s32[512]{0:T(512)} %bitcast.135, f32[512,128]{1,0:T(8,128)S(1)} %get-tuple-element.51, f32[]{:T(128)} %constant.252.clone.1), kind=kCustom, calls=%fused_computation.96 | custom fusion | flops 65536 | bytes 33280 | tf_op jit(solution)/shard_map/scatter-add | solution.py:119
  383.3 1.3 collective-permute-start.2
  385.2 3.4 scatter_fusion
  388.6 6.4 %scatter_custom_fusion.3 = f32[256,128]{1,0:T(8,128)S(1)} fusion(s32[704]{0:T(1024)S(1)} %reshape.617, f32[704,128]{1,0:T(8,128)S(1)} %reshape.619, f32[]{:T(128)} %constant.252.clone.1), kind=kCustom, calls=%fused_computation.83 | custom fusion | flops 90112 | bytes 131076 | tf_op jit(solution)/shard_map/scatter-add | solution.py:132
  (145 shorter events, 33.4 us)
Async XLA Ops:
  0.6 30.3 %copy-start.19 = (f32[3]{0:T(128)S(1)}, f32[3]{0:T(128)}, u32[]{:S(2)}) copy-start(f32[3]{0:T(128)} %param.9) | copy-start | bytes 40
  3.2 29.1 %copy-start.17 = (pred[512]{0:T(512)(128)(4,1)}, pred[512]{0:T(512)(128)(4,1)S(1)}, u32[]{:S(2)}) copy-start(pred[512]{0:T(512)(128)(4,1)S(1)} %get-tuple-element.63) | copy-start | bytes 1540
  10.4 22.7 %all-to-all-start = ((s32[32,1,22]{2,1,0:T(1,128)}), s32[32,1,22]{2,1,0:T(1,128)S(1)}, u32[]{:S(2)}, u32[]{:S(2)}) async-start(s32[32,1,22]{2,1,0:T(1,128)} %bitcast.6), calls=%async_computation | async-start | bytes 32768 | tf_op jit(solution)/shard_map/all_to_all | solution.py:88
  21.6 37.2 %collective-permute-start = (f32[64,2]{1,0:T(8,128)S(1)}, f32[64,2]{1,0:T(8,128)S(1)}, u32[]{:S(2)}, u32[]{:S(2)}) collective-permute-start(f32[64,2]{1,0:T(8,128)S(1)} %slice.177), channel_id=1, source_target_pairs={{0,32},{32,64},{64,96},{96,128},{128,160},{160,192},{192,224},{224... | collective-permute-start | bytes 1544 | tf_op jit(solution)/shard_map/ppermute | solution.py:14
  24.8 224.1 %collective-permute-start.1 = (f32[64,128]{1,0:T(8,128)}, f32[64,128]{1,0:T(8,128)}, u32[]{:S(2)}, u32[]{:S(2)}) collective-permute-start(f32[64,128]{1,0:T(8,128)} %slice.151), channel_id=1, source_target_pairs={{0,32},{32,64},{64,96},{96,128},{128,160},{160,192},{192,224},{224... | collective-permute-start | bytes 98312 | tf_op jit(solution)/shard_map/ppermute | solution.py:14
  33.1 25.7 %copy-start.14 = (s32[1024]{0:T(1024)}, s32[1024]{0:T(1024)S(1)}, u32[]{:S(2)}) copy-start(s32[1024]{0:T(1024)S(1)} %pad_clamp_fusion) | copy-start | bytes 12292
  35.0 10.9 %copy-start = (f32[256,128]{1,0:T(8,128)S(1)}, f32[256,128]{1,0:T(8,128)}, u32[]{:S(2)}) copy-start(f32[256,128]{1,0:T(8,128)} %param.6) | copy-start | bytes 393220
  35.9 15.2 %all-to-all-start.1 = ((f32[32,22,2]{1,2,0:T(2,128)}), f32[32,22,2]{1,2,0:T(2,128)S(1)}, u32[]{:S(2)}, u32[]{:S(2)}) async-start(f32[32,22,2]{1,2,0:T(2,128)} %copy.64), calls=%async_computation.1 | async-start | bytes 65536 | tf_op jit(solution)/shard_map/all_to_all | solution.py:91
  51.1 196.7 %all-to-all-start.2 = ((f32[32,22,128]{2,1,0:T(8,128)}), f32[32,22,128]{2,1,0:T(8,128)}, u32[]{:S(2)}, u32[]{:S(2)}) async-start(f32[32,22,128]{2,1,0:T(8,128)} %reshape.576), calls=%async_computation.2 | async-start | bytes 786432 | tf_op jit(solution)/shard_map/all_to_all | solution.py:90
  60.0 1.6 copy-start.10
  60.0 1.6 copy-start.12
  61.6 23.6 %copy-start.6 = (pred[128,128]{1,0:T(8,128)(4,1)S(1)}, pred[128,128]{1,0:T(8,128)(4,1)}, u32[]{:S(2)}) copy-start(pred[128,128]{1,0:T(8,128)(4,1)} %iota_compare_fusion.3) | copy-start | bytes 49156
  105.3 69.4 %copy-start.8 = (pred[128,128]{1,0:T(8,128)(4,1)S(1)}, pred[128,128]{1,0:T(8,128)(4,1)}, u32[]{:S(2)}) copy-start(pred[128,128]{1,0:T(8,128)(4,1)} %iota_compare_fusion.6) | copy-start | bytes 49156
  175.1 0.7 copy-start.22
  175.8 68.3 %copy-start.2 = (f32[128,384]{1,0:T(8,128)S(1)}, f32[128,384]{1,0:T(8,128)}, u32[]{:S(2)}) copy-start(f32[128,384]{1,0:T(8,128)} %get-tuple-element.50) | copy-start | bytes 589828
  175.8 68.9 %copy-start.3 = (f32[128,384]{1,0:T(8,128)S(1)}, f32[128,384]{1,0:T(8,128)}, u32[]{:S(2)}) copy-start(f32[128,384]{1,0:T(8,128)} %get-tuple-element.49) | copy-start | bytes 589828
  244.1 1.6 copy-start.4
  246.3 3.3 copy-start.15
  255.1 2.2 copy-start.18
  255.1 2.2 copy-start.20
  255.1 2.2 copy-start.21
  257.7 11.1 %copy-start.1 = (f32[2,384,384]{2,1,0:T(8,128)S(1)}, f32[2,384,384]{2,1,0:T(8,128)}, u32[]{:S(2)}) copy-start(f32[2,384,384]{2,1,0:T(8,128)} %fusion.1) | copy-start | bytes 3538948
  257.7 11.1 %copy-start.7 = (pred[384,384]{1,0:T(8,128)(4,1)S(1)}, pred[384,384]{1,0:T(8,128)(4,1)}, u32[]{:S(2)}) copy-start(pred[384,384]{1,0:T(8,128)(4,1)} %iota_compare_fusion.1) | copy-start | bytes 442372
  257.7 11.1 %copy-start.11 = (f32[2,384]{1,0:T(2,128)S(1)}, f32[2,384]{1,0:T(2,128)}, u32[]{:S(2)}) copy-start(f32[2,384]{1,0:T(2,128)} %copy-done.10) | copy-start | bytes 9220
  257.7 11.1 %copy-start.13 = (f32[2,384]{1,0:T(2,128)S(1)}, f32[2,384]{1,0:T(2,128)}, u32[]{:S(2)}) copy-start(f32[2,384]{1,0:T(2,128)} %copy-done.12) | copy-start | bytes 9220
  261.4 127.1 %all-to-all-start.3 = ((f32[32,22,128]{2,1,0:T(8,128)}), f32[32,22,128]{2,1,0:T(8,128)S(1)}, u32[]{:S(2)}, u32[]{:S(2)}) async-start(f32[32,22,128]{2,1,0:T(8,128)} %reshape.536), calls=%async_computation.3 | async-start | bytes 786432 | tf_op jit(solution)/shard_map/all_to_all | solution.py:131
  268.8 2.5 copy-start.9
  268.8 116.3 %copy-start.16 = (s32[512,1]{0,1:T(1,128)S(1)}, s32[512,1]{0,1:T(1,128)}, u32[]{:S(2)}) copy-start(s32[512,1]{0,1:T(1,128)} %get-tuple-element.59) | copy-start | bytes 6148
  383.3 11.7 %collective-permute-start.2 = (f32[64,128]{1,0:T(8,128)S(1)}, f32[64,128]{1,0:T(8,128)S(1)}, u32[]{:S(2)}, u32[]{:S(2)}) collective-permute-start(f32[64,128]{1,0:T(8,128)S(1)} %scatter_custom_fusion.4), channel_id=1, source_target_pairs={{32,0},{64,32},{96,64},{128,96},{160,128},{192,160},{224,192},{256... | collective-permute-start | bytes 98312 | tf_op jit(solution)/shard_map/ppermute | solution.py:14
  395.1 0.7 copy-start.5
where the time goes:
time: 401 us; the launch traced here: 396 us
  other arithmetic  200 us (50%)
  blocking collectives  108 us (27%)
  starting transfers between devices  40.2 us (10%)
  local copies, waits for them, and re-layouts  29.4 us (7%)
  matrix products  14.4 us (4%)
    another operation x14, other arithmetic, block_grads(): factor = jnp.linalg.cholesky(kernel)  112 us
    psum x1, blocking collectives, shards(): theta_total = lax.psum(grad_theta, ('band', 'region'))  108 us
    another operation x4, other arithmetic, block_grads(): inverse = jax.scipy.linalg.solve_triangular(factor, identity, lower=True)  60.8 us
    all_to_all x1, starting transfers between devices, shards(): lax.all_to_all(requests, 'region', split_axis=0, concat_axis=0, tiled=True)  10.4 us
    another operation x11, local copies, waits for them, and re-layouts  8.55 us
  transfers between devices with their start and end apart: 7, of which 1 were waited for; matrix products, arithmetic and copies ran while one was open for 56% of the time, Pallas kernels for 0%

commit v1 on v0

v1 whole, which is shorter than its diff:
```python
import functools

import jax
import jax.numpy as jnp
from jax import lax
from jax.experimental import pallas as pl
from jax.experimental.pallas import tpu as pltpu
from jax.sharding import PartitionSpec as P

MESH = pl.DeviceIdType.MESH
F32 = jnp.float32
BF16 = jnp.bfloat16
M = 256
RIM = 64
POOL = 160
STEPS_A = (0, 6, 1)
STEPS_S = (0, 6, 1)


def split(x, parts):
    out = []
    for _ in range(parts - 1):
        high = x.astype(BF16)
        out.append(high)
        x = x - high.astype(F32)
    out.append(x.astype(BF16))
    return out


def nn(a, b):
    return lax.dot_general(a, b, (((1,), (0,)), ((), ())), preferred_element_type=F32)


def nt(a, b):
    return lax.dot_general(a, b, (((1,), (1,)), ((), ())), preferred_element_type=F32)


def tn(a, b):
    return lax.dot_general(a, b, (((0,), (0,)), ((), ())), preferred_element_type=F32)


def one_pass(a, b):
    return nn(a.astype(BF16), b.astype(BF16))


def three_pass(a, b, dot=nn):
    a_high, a_low = split(a, 2)
    b_high, b_low = split(b, 2)
    return dot(a_high, b_high) + (dot(a_high, b_low) + dot(a_low, b_high))


def full(a, b):
    return jnp.dot(a, b, precision=lax.Precision.HIGHEST, preferred_element_type=F32)


def picked(dot, chosen, x, parts):
    return sum(dot(chosen, part) for part in reversed(split(x, parts)))


def iota(shape, dim):
    return lax.broadcasted_iota(jnp.int32, shape, dim)


def inverses(mats, refs, lowest, steps):
    n = mats[0].shape[0]
    eye = (iota((n, n), 0) == iota((n, n), 1)).astype(F32)
    lows = []
    for mat, ref in zip(mats, refs):
        sums = jnp.sum(jnp.abs(mat), axis=0, keepdims=True)
        top = jnp.max(sums, axis=1, keepdims=True) * 1.0001
        low = lowest / top
        scale = 2.0 / (top + lowest)
        ref[...] = (2.0 * scale) * eye - (scale * scale) * mat
        lows.append(4.0 * low / ((1.0 + low) * (1.0 + low)))

    def step(first, second, lows):
        later = []
        products = [first(mat, ref[...]) for mat, ref in zip(mats, refs)]
        for product, ref, low in zip(products, refs, lows):
            scale = 2.0 / (1.0 + low)
            held = ref[...]
            ref[...] = held + second(held, (2.0 * scale - 1.0) * eye - (scale * scale) * product)
            later.append(4.0 * low / ((1.0 + low) * (1.0 + low)))
        return later

    for count, first, second in zip(steps, (one_pass, three_pass, full), (one_pass, three_pass, three_pass)):
        if count:
            lows = lax.fori_loop(0, count, lambda i, l, f=first, s=second: tuple(step(f, s, l)), tuple(lows))
    return [ref[...] for ref in refs]


def kernel(
    n_band, n_reg, slots,
    values_ref, coords_ref, near_ref, params_ref,
    grad_ref, theta_ref,
    ask_out, ask_in, rows_out, rows_in, back_out, back_in,
    rim_out, rim_in, rimback_out, rimback_in,
    th_out, th_in, tb_out, tb_in,
    chosen_ref, spread_ref, sel_ref, kern_ref, shape_ref, slope_ref, inv_a0, inv_a1, inv_s0, inv_s1,
    send_sems, recv_sems,
):
    band, reg = lax.axis_index("band"), lax.axis_index("region")
    points, reps = values_ref.shape
    blocks, width = near_ref.shape
    length = points // blocks
    half = points // 2
    order_n = width + length
    rim_start = points - RIM

    def region_peer(i):
        return lax.rem(reg + i, n_reg)

    def band_peer(i):
        return lax.rem(band + i, n_band)

    barrier = pltpu.get_barrier_semaphore()

    def greet_region(i, c):
        pl.semaphore_signal(barrier, inc=1, device_id=(band, region_peer(i)), device_id_type=MESH)
        return c

    def greet_band(i, c):
        pl.semaphore_signal(barrier, inc=1, device_id=(band_peer(i), reg), device_id_type=MESH)
        return c

    lax.fori_loop(1, n_reg, greet_region, 0)
    lax.fori_loop(1, n_band, greet_band, 0)

    def to_peers(out, into, stage):
        def send(i, c):
            peer = region_peer(i)
            pltpu.make_async_remote_copy(
                src_ref=out.at[peer], dst_ref=into.at[reg],
                send_sem=send_sems.at[stage], recv_sem=recv_sems.at[stage],
                device_id=(band, peer), device_id_type=MESH,
            ).start()
            return c
        lax.fori_loop(1, n_reg, send, 0)

    def from_peers(out, into, stage):
        some = pl.ds(0, n_reg - 1)
        return pltpu.make_async_remote_copy(
            src_ref=out.at[some], dst_ref=into.at[some],
            send_sem=send_sems.at[stage], recv_sem=recv_sems.at[stage],
            device_id=(band, region_peer(1)), device_id_type=MESH,
        )

    near = near_ref[...]
    owner = near // points
    offset = near - owner * points
    owner_band = owner // n_reg
    owner_reg = owner - owner_band * n_reg
    is_rim = owner_band == band - 1
    is_own = jnp.logical_and(owner_band == band, owner_reg == reg)
    is_far = jnp.logical_and(owner_band == band, owner_reg != reg)
    far_row = jnp.where(is_far, owner_reg, -1)
    table_row = jnp.where(is_rim, n_reg, owner_reg)
    off_t = [(iota((points, width), 0) == offset[b : b + 1]).astype(BF16) for b in range(blocks)]
    far_t = [(iota((n_reg, width), 0) == far_row[b : b + 1]).astype(F32) for b in range(blocks)]
    counts = sum(nt(far_t[b].astype(BF16), off_t[b]) for b in range(blocks))
    mask = (counts > 0.5).astype(F32)
    below = (iota((points, points), 0) < iota((points, points), 1)).astype(BF16)
    rank = nn(mask.astype(BF16), below)

    x_row, y_row = coords_ref[0:1, :], coords_ref[1:2, :]
    ask_out[:, 0, :] = mask[:, :half]
    ask_out[:, 1, :] = mask[:, half:]
    for k, part in enumerate((x_row[:, :half], x_row[:, half:], y_row[:, :half], y_row[:, half:])):
        ask_out[:, 2 + k, :] = jnp.broadcast_to(part, (n_reg, half))
    ask_out[:, 6, :] = jnp.zeros((n_reg, half), F32)
    ask_out[:, 7, :] = jnp.zeros((n_reg, half), F32)
    rim_out[0:RIM, :] = values_ref[rim_start:, :]
    rim_out[RIM : RIM + 8, :] = jnp.concatenate(
        [x_row[:, half:], y_row[:, half:], jnp.zeros((6, half), F32)], axis=0
    )

    pl.semaphore_wait(barrier, n_reg + n_band - 2)
    to_peers(ask_out, ask_in, 0)
    rim_copy = pltpu.make_async_remote_copy(
        src_ref=rim_out, dst_ref=rim_in, send_sem=send_sems.at[4], recv_sem=recv_sems.at[4],
        device_id=(band_peer(1), reg), device_id_type=MESH,
    )
    rim_copy.start()
    ask_in[pl.ds(reg, 1)] = ask_out[pl.ds(reg, 1)]
    rows_in[pl.ds(reg, 1)] = jnp.zeros((1, slots, reps), F32)
    back_in[pl.ds(reg, 1)] = jnp.zeros((1, slots, reps), F32)

    rank_bf = rank.astype(BF16)
    index_rows = []
    for b in range(blocks):
        slot = jnp.sum(far_t[b] * nn(rank_bf, off_t[b]), axis=0, keepdims=True).astype(jnp.int32)
        far_index = points + RIM + owner_reg[b : b + 1] * slots + slot
        rim_index = points + offset[b : b + 1] - rim_start
        index_rows.append(
            jnp.where(is_own[b : b + 1], offset[b : b + 1], jnp.where(is_rim[b : b + 1], rim_index, far_index))
        )
    table = chosen_ref.shape[2]
    index_cols = jnp.concatenate(index_rows + [jnp.zeros((8 - blocks, width), jnp.int32)], axis=0).astype(F32).T
    for b in range(blocks):
        column = index_cols[:, b : b + 1].astype(jnp.int32)
        chosen_ref[b] = (iota((width, table), 1) == column).astype(BF16)
        spread_ref[b] = (iota((table, width), 0) == index_rows[b]).astype(BF16)

    from_peers(ask_out, ask_in, 0).wait_recv()
    rim_copy.wait_recv()

    wanted = jnp.concatenate([ask_in[:, 0, :], ask_in[:, 1, :]], axis=1)
    wanted_rank = nn(wanted.astype(BF16), below)
    slot_of = jnp.where(wanted > 0.5, wanted_rank, -1.0)
    sel = (
        jnp.broadcast_to(slot_of[:, None, :], (n_reg, slots, points))
        == iota((n_reg, slots, points), 1).astype(F32)
    )
    sel_ref[...] = sel.astype(F32).reshape(n_reg * slots, points).astype(BF16)
    rows_out[...] = picked(nn, sel_ref[...], values_ref[...], 3).reshape(n_reg, slots, reps)
    to_peers(rows_out, rows_in, 1)

    zero_half = jnp.zeros((1, half), F32)
    tables = []
    for k in range(2):
        peers = jnp.concatenate([ask_in[:, 2 + 2 * k, :], ask_in[:, 3 + 2 * k, :]], axis=1)
        rim_row = jnp.concatenate([zero_half, rim_in[RIM + k : RIM + k + 1, :]], axis=1)
        tables += [peers, rim_row, jnp.zeros((7, points), F32)]
    coord_table = jnp.concatenate(tables, axis=0)
    rows = n_reg + 8
    variance = jnp.exp(jnp.full((1, 1), params_ref[0], F32))
    inverse_range = jnp.sqrt(jnp.full((1, 1), 3.0, F32)) * jnp.exp(jnp.full((1, 1), -params_ref[1], F32))
    nugget = jnp.exp(jnp.full((1, 1), params_ref[2], F32))
    parts = split(coord_table, 3)
    for b in range(blocks):
        own_t = (iota((rows, width), 0) == table_row[b : b + 1]).astype(F32)
        found = sum(nn(part, off_t[b]) for part in reversed(parts))
        x_near = jnp.sum(own_t * found[:rows], axis=0, keepdims=True)
        y_near = jnp.sum(own_t * found[rows:], axis=0, keepdims=True)
        here = slice(b * length, (b + 1) * length)
        x_joint = jnp.concatenate([x_near, x_row[:, here]], axis=1)
        y_joint = jnp.concatenate([y_near, y_row[:, here]], axis=1)
        cols = jnp.concatenate([x_joint, y_joint, jnp.zeros((6, order_n), F32)], axis=0).T
        delta_x = cols[:, 0:1] - x_joint
        delta_y = cols[:, 1:2] - y_joint
        scaled = inverse_range * jnp.sqrt(delta_x * delta_x + delta_y * delta_y)
        decayed = variance * jnp.exp(-scaled)
        shape_part = decayed + scaled * decayed
        shape_ref[b] = shape_part
        slope_ref[b] = scaled * scaled * decayed
        diagonal = iota((order_n, order_n), 0) == iota((order_n, order_n), 1)
        kern_ref[b] = jnp.where(diagonal, shape_part + nugget, shape_part)

    all_blocks = range(blocks)
    inv_a = inverses([kern_ref[b, :width, :width] for b in all_blocks], [inv_a0, inv_a1], nugget, STEPS_A)
    x_t = [full(kern_ref[b, width:, :width], inv_a[b]) for b in all_blocks]
    x_n = [full(inv_a[b], kern_ref[b, :width, width:]) for b in all_blocks]
    schur = [kern_ref[b, width:, width:] - full(x_t[b], kern_ref[b, :width, width:]) for b in all_blocks]
    inv_s = inverses(schur, [inv_s0, inv_s1], nugget, STEPS_S)

    from_peers(rows_out, rows_in, 1).wait_recv()
    pad = table - points - RIM - n_reg * slots
    value_table = jnp.concatenate(
        [values_ref[...], rim_in[0:RIM, :], rows_in[...].reshape(n_reg * slots, reps), jnp.zeros((pad, reps), F32)],
        axis=0,
    )
    value_parts = split(value_table, 3)
    heads, us, backs, spread = [], [], [], 0.0
    for b in all_blocks:
        y_near = sum(nn(chosen_ref[b], part) for part in reversed(value_parts))
        here = slice(b * length, (b + 1) * length)
        resid = values_ref[here, :] - full(x_t[b], y_near)
        u = full(inv_s[b], resid)
        back_head = full(x_n[b], u)
        heads.append(three_pass(inv_a[b], y_near))
        us.append(u)
        backs.append(back_head)
        spread = spread + picked(nn, spread_ref[b], back_head, 3)
    back_out[...] = spread[points + RIM : points + RIM + n_reg * slots].reshape(n_reg, slots, reps)
    to_peers(back_out, back_in, 2)
    rimback_out[...] = spread[points : points + RIM]
    rimback_copy = pltpu.make_async_remote_copy(
        src_ref=rimback_out, dst_ref=rimback_in, send_sem=send_sems.at[5], recv_sem=recv_sems.at[5],
        device_id=(band_peer(n_band - 1), reg), device_id_type=MESH,
    )
    rimback_copy.start()
    grad_ref[...] = spread[:points] - jnp.concatenate(us, axis=0)

    sums = [jnp.zeros((1, 1), F32)] * 3
    for b in all_blocks:
        u, head_back = us[b], -backs[b]
        back = jnp.concatenate([head_back, u], axis=0)
        left = jnp.concatenate([heads[b] + 0.5 * head_back, 0.5 * u], axis=0)
        v = jnp.concatenate(
            [-x_n[b], (iota((length, length), 0) == iota((length, length), 1)).astype(F32)], axis=0
        )
        vs = (-0.5 * reps) * jnp.concatenate([-three_pass(x_n[b], inv_s[b]), inv_s[b]], axis=0)
        left = jnp.concatenate([left, vs], axis=1)
        right = jnp.concatenate([back, v], axis=1)
        grad_kernel = three_pass(left, right, nt)
        total = lambda z: jnp.sum(jnp.sum(z, axis=0, keepdims=True), axis=1, keepdims=True)
        sums = [
            sums[0] + total(grad_kernel * shape_ref[b]),
            sums[1] + total(grad_kernel * slope_ref[b]),
            sums[2] + nugget * total(left * right),
        ]
    lane = iota((1, half), 1)
    mine = jnp.where(lane == 0, sums[0], jnp.where(lane == 1, sums[1], jnp.where(lane == 2, sums[2], 0.0)))
    th_out[...] = mine

    def send_region(i, c):
        pltpu.make_async_remote_copy(
            src_ref=th_out, dst_ref=th_in.at[reg], send_sem=send_sems.at[3], recv_sem=recv_sems.at[3],
            device_id=(band, region_peer(i)), device_id_type=MESH,
        ).start()
        return c

    lax.fori_loop(1, n_reg, send_region, 0)
    th_in[pl.ds(reg, 1)] = mine[None]
    from_theta = pltpu.make_async_remote_copy(
        src_ref=th_in.at[pl.ds(0, n_reg - 1)], dst_ref=th_in.at[pl.ds(0, n_reg - 1)],
        send_sem=send_sems.at[3], recv_sem=recv_sems.at[3],
        device_id=(band, region_peer(1)), device_id_type=MESH,
    )
    from_theta.wait_recv()
    band_sum = jnp.sum(th_in[...], axis=0)
    tb_out[...] = band_sum

    def send_band(i, c):
        pltpu.make_async_remote_copy(
            src_ref=tb_out, dst_ref=tb_in.at[band], send_sem=send_sems.at[6], recv_sem=recv_sems.at[6],
            device_id=(band_peer(i), reg), device_id_type=MESH,
        ).start()
        return c

    lax.fori_loop(1, n_band, send_band, 0)
    tb_in[pl.ds(band, 1)] = band_sum[None]

    from_peers(back_out, back_in, 2).wait_recv()
    returned = back_in[...].reshape(n_reg * slots, reps)
    grad_ref[...] += picked(tn, sel_ref[...], returned, 3)
    rimback_copy.wait_recv()
    grad_ref[rim_start:, :] += rimback_in[...]

    from_bands = pltpu.make_async_remote_copy(
        src_ref=tb_in.at[pl.ds(0, n_band - 1)], dst_ref=tb_in.at[pl.ds(0, n_band - 1)],
        send_sem=send_sems.at[6], recv_sem=recv_sems.at[6],
        device_id=(band_peer(1), reg), device_id_type=MESH,
    )
    from_bands.wait_recv()
    theta_ref[...] = jnp.sum(tb_in[...], axis=0) * (1.0 / (points * n_band * n_reg * reps))

    from_peers(ask_out, ask_in, 0).wait_send()
    from_peers(rows_out, rows_in, 1).wait_send()
    from_peers(back_out, back_in, 2).wait_send()
    from_theta.wait_send()
    from_bands.wait_send()
    rim_copy.wait_send()
    rimback_copy.wait_send()


def shards(n_band, n_reg, values, coords, neighbours, log_params):
    points, reps = values.shape
    blocks, width = neighbours.shape
    length = points // blocks
    order_n = width + length
    cap = (2 * POOL + n_reg - 2) // (n_reg - 1)
    slots = -(-cap // 16) * 16
    table = -(-(points + RIM + n_reg * slots) // 128) * 128
    half = points // 2
    vmem = lambda *shape: pltpu.VMEM(shape, F32)
    grad, theta = pl.pallas_call(
        functools.partial(kernel, n_band, n_reg, slots),
        out_shape=(jax.ShapeDtypeStruct((points, reps), F32), jax.ShapeDtypeStruct((1, half), F32)),
        in_specs=[pl.BlockSpec(memory_space=pltpu.VMEM)] * 3 + [pl.BlockSpec(memory_space=pltpu.SMEM)],
        out_specs=(pl.BlockSpec(memory_space=pltpu.VMEM), pl.BlockSpec(memory_space=pltpu.VMEM)),
        scratch_shapes=[
            vmem(n_reg, 8, half), vmem(n_reg, 8, half),
            vmem(n_reg, slots, reps), vmem(n_reg, slots, reps),
            vmem(n_reg, slots, reps), vmem(n_reg, slots, reps),
            vmem(RIM + 8, reps), vmem(RIM + 8, reps), vmem(RIM, reps), vmem(RIM, reps),
            vmem(1, half), vmem(n_reg, 1, half), vmem(1, half), vmem(n_band, 1, half),
            pltpu.VMEM((blocks, width, table), BF16), pltpu.VMEM((blocks, table, width), BF16),
            pltpu.VMEM((n_reg * slots, points), BF16),
            vmem(blocks, order_n, order_n), vmem(blocks, order_n, order_n), vmem(blocks, order_n, order_n),
            vmem(width, width), vmem(width, width), vmem(length, length), vmem(length, length),
            pltpu.SemaphoreType.DMA((7,)), pltpu.SemaphoreType.DMA((7,)),
        ],
        compiler_params=pltpu.CompilerParams(
            collective_id=0, has_side_effects=True, vmem_limit_bytes=48 * 1024 * 1024
        ),
    )(values, coords, neighbours, log_params)
    return grad, theta[0, :3]


def solution(mesh):
    placed = (
        P(("band", "region"), None),
        P(None, ("band", "region")),
        P(("band", "region"), None),
        P(),
    )
    return jax.shard_map(
        functools.partial(shards, mesh.shape["band"], mesh.shape["region"]),
        mesh=mesh,
        in_specs=placed,
        out_specs=(P(("band", "region"), None), P()),
        check_vma=False,
    )
```

time: 401 us -> 55.7 us (0.14); the launches traced: 396 us -> 55.5 us
  other arithmetic: 200 us -> 0 us
  blocking collectives: 108 us -> 0 us
  Pallas kernels: 0 us -> 50.8 us
  starting transfers between devices: 40.2 us -> 0 us
  local copies, waits for them, and re-layouts: 29.4 us -> 4.08 us
  matrix products: 14.4 us -> 0 us
    another operation x20 -> x0, other arithmetic: 174 us -> none  [the longest x14 112 us: block_grads(): factor = jnp.linalg.cholesky(kernel)]
    psum x1 -> x0, blocking collectives: 108 us -> none  [shards(): theta_total = lax.psum(grad_theta, ('band', 'region'))]
    pallas_call x0 -> x1, Pallas kernels: none -> 50.8 us  [shards(): pl.pallas_call(functools.partial(kernel, n_band, n_reg, slots), out_shape...]
    all_to_all x4 -> x0, starting transfers between devices: 33 us -> none  [the longest x1 10.4 us: shards(): lax.all_to_all(requests, 'region', split_axis=0, concat_axis=0, tiled=True)]
    scatter-add x5 -> x0, other arithmetic: 16.9 us -> none  [the longest x1 6.39 us: shards(): jax.ops.segment_sum(returned.reshape(-1, reps), requested.reshape(-1), po...]
    another operation x17 -> x0, local copies, waits for them, and re-layouts: 9.56 us -> none
    dot_general x7 -> x0, matrix products: 8.53 us -> none  [the longest x1 2.32 us: block_grads(): jnp.dot(tail_inv.T, tail_inv, precision=highest)]
    ppermute x3 -> x0, starting transfers between devices: 7.21 us -> none  [passed_along(): return lax.ppermute(x, axis, pairs)]
  transfers between devices with their start and end apart: 7 -> 0, of which waited for: 1 -> 0; matrix products, arithmetic and copies ran while one was open for 56% -> 0% of each run, Pallas kernels for 0% -> 0%
where the time goes in v1:
time: 55.7 us; the launch traced here: 55.5 us
  Pallas kernels  50.8 us (91%)
  local copies, waits for them, and re-layouts  4.08 us (7%)
  between operations  0.65 us (1%)
    pallas_call x1, Pallas kernels, shards(): pl.pallas_call(functools.partial(kernel, n_band, n_reg, slots), out_shape...  50.8 us
    unnamed x9, local copies, waits for them, and re-layouts  3.57 us

profile of v1, /device:TPU:1, one launch (start us, length us, event | category | flops | bytes accessed | tf_op | source)
XLA Modules:
  0.0 55.5 jit_solution(12980961316850788379)
XLA Ops:
  0.6 0.0 copy-start
  0.6 0.9 %copy-done = f32[256,128]{1,0:T(8,128)S(1)} copy-done((f32[256,128]{1,0:T(8,128)S(1)}, f32[256,128]{1,0:T(8,128)}, u32[]{:S(2)}) %copy-start) | copy-done | bytes 131096
  1.5 0.0 copy-start.1
  1.5 0.7 %copy-done.1 = f32[2,256]{1,0:T(2,128)S(1)} copy-done((f32[2,256]{1,0:T(2,128)S(1)}, f32[2,256]{1,0:T(2,128)}, u32[]{:S(2)}) %copy-start.1) | copy-done | bytes 2072
  2.2 0.0 copy-start.2
  2.2 0.7 %copy-done.2 = s32[2,256]{1,0:T(2,128)S(1)} copy-done((s32[2,256]{1,0:T(2,128)S(1)}, s32[2,256]{1,0:T(2,128)}, u32[]{:S(2)}) %copy-start.2) | copy-done | bytes 2072
  2.9 0.0 copy-start.3
  2.9 0.7 %copy-done.3 = f32[3]{0:T(128)S(1)} copy-done((f32[3]{0:T(128)S(1)}, f32[3]{0:T(128)}, u32[]{:S(2)}) %copy-start.3) | copy-done | bytes 36
  3.6 50.8 %shard_map.59 = (f32[256,128]{1,0:T(8,128)S(1)}, f32[1,128]{1,0:T(1,128)S(1)}) custom-call(f32[256,128]{1,0:T(8,128)S(1)} %copy-done, f32[2,256]{1,0:T(2,128)S(1)} %copy-done.1, s32[2,256]{1,0:T(2,128)S(1)} %copy-done.2, f32[3]{0:T(128)S(1)} %copy-done.3), custom_call_target="tpu_custom_call" | custom-call | tf_op jit(solution)/shard_map/pallas_call | solution.py:367
  54.3 0.5 slice_bitcast_fusion
  54.8 0.7 %copy.7 = f32[256,128]{1,0:T(8,128)} copy(f32[256,128]{1,0:T(8,128)S(1)} %get-tuple-element.8) | data formatting | bytes 262144
Async XLA Ops:
  0.6 0.9 %copy-start = (f32[256,128]{1,0:T(8,128)S(1)}, f32[256,128]{1,0:T(8,128)}, u32[]{:S(2)}) copy-start(f32[256,128]{1,0:T(8,128)} %values_ref.1) | copy-start | bytes 393220
  1.5 0.7 %copy-start.1 = (f32[2,256]{1,0:T(2,128)S(1)}, f32[2,256]{1,0:T(2,128)}, u32[]{:S(2)}) copy-start(f32[2,256]{1,0:T(2,128)} %coords_ref.1) | copy-start | bytes 6148
  2.2 0.7 %copy-start.2 = (s32[2,256]{1,0:T(2,128)S(1)}, s32[2,256]{1,0:T(2,128)}, u32[]{:S(2)}) copy-start(s32[2,256]{1,0:T(2,128)} %near_ref.1) | copy-start | bytes 6148
  2.9 0.7 %copy-start.3 = (f32[3]{0:T(128)S(1)}, f32[3]{0:T(128)}, u32[]{:S(2)}) copy-start(f32[3]{0:T(128)} %params_ref.1) | copy-start | bytes 40

commit v2 on v1

v2 whole, which is shorter than its diff:
```python
import functools

import jax
import jax.numpy as jnp
from jax import lax
from jax.experimental import pallas as pl
from jax.experimental.pallas import tpu as pltpu
from jax.sharding import PartitionSpec as P

MESH = pl.DeviceIdType.MESH
F32 = jnp.float32
BF16 = jnp.bfloat16
M = 256
RIM = 64
POOL = 160


def split(x, parts):
    out = []
    for _ in range(parts - 1):
        high = x.astype(BF16)
        out.append(high)
        x = x - high.astype(F32)
    out.append(x.astype(BF16))
    return out


def nn(a, b):
    return lax.dot_general(a, b, (((1,), (0,)), ((), ())), preferred_element_type=F32)


def nt(a, b):
    return lax.dot_general(a, b, (((1,), (1,)), ((), ())), preferred_element_type=F32)


def tn(a, b):
    return lax.dot_general(a, b, (((0,), (0,)), ((), ())), preferred_element_type=F32)


def three_pass(a, b, dot=nn):
    a_high, a_low = split(a, 2)
    b_high, b_low = split(b, 2)
    return dot(a_high, b_high) + (dot(a_high, b_low) + dot(a_low, b_high))


def full(a, b):
    return jnp.dot(a, b, precision=lax.Precision.HIGHEST, preferred_element_type=F32)


def picked(dot, chosen, x, parts):
    return sum(dot(chosen, part) for part in reversed(split(x, parts)))


def iota(shape, dim):
    return lax.broadcasted_iota(jnp.int32, shape, dim)


def inverses(mats, refs, lowest, carried):
    n = mats[0].shape[0]
    eye = (iota((n, n), 0) == iota((n, n), 1)).astype(F32)

    def factor_of(product, low):
        scale = 2.0 / (1.0 + low)
        return (2.0 * scale) * eye - (scale * scale) * product

    def raised(low):
        return 4.0 * low / ((1.0 + low) * (1.0 + low))

    lows, factors, starts = [], [], []
    for mat in mats:
        sums = jnp.sum(jnp.abs(mat), axis=0, keepdims=True)
        over = 1.0 / (jnp.max(sums, axis=1, keepdims=True) * 1.0001)
        low = lowest * over
        start = over * mat
        factor = factor_of(start, low)
        starts.append(start)
        factors.append(factor)
        lows.append(raised(low))
    products = [three_pass(start, factor) for start, factor in zip(starts, factors)]
    for mat, ref, factor, product in zip(mats, refs, factors, products):
        over = jnp.max(jnp.sum(jnp.abs(mat), axis=0, keepdims=True), axis=1, keepdims=True) * 1.0001
        ref[:n] = factor / over
        ref[n:] = product

    def step(i, lows):
        held = [ref[...] for ref in refs]
        factors = [factor_of(both[n:], low) for both, low in zip(held, lows)]
        both = [three_pass(x, factor) for x, factor in zip(held, factors)]
        for ref, x in zip(refs, both):
            ref[...] = x
        return tuple(raised(low) for low in lows)

    lows = lax.fori_loop(0, carried, step, tuple(lows))
    found = [ref[:n] for ref in refs]
    products = [three_pass(mat, x) for mat, x in zip(mats, found)]
    found = [three_pass(x, factor_of(product, low)) for x, product, low in zip(found, products, lows)]
    lows = [raised(low) for low in lows]
    products = [full(mat, x) for mat, x in zip(mats, found)]
    return [
        x + three_pass(x, factor_of(product, low) - eye) for x, product, low in zip(found, products, lows)
    ]


def kernel(
    n_band, n_reg, slots,
    values_hbm, coords_hbm, near_hbm, params_hbm,
    grad_ref, theta_ref,
    values_ref, coords_ref, near_ref, params_ref,
    place_in, ask_out, ask_in, rows_out, rows_in, back_out, back_in,
    rimplace_in, rim_in, rimback_out, rimback_in,
    th_out, th_in, tb_out, tb_in,
    chosen_ref, spread_ref, sel_ref, kern_ref, shape_ref, slope_ref, inv_a0, inv_a1, inv_s0, inv_s1,
    local_sems, send_sems, recv_sems, known_sems,
):
    band, reg = lax.axis_index("band"), lax.axis_index("region")
    points, reps = values_ref.shape
    blocks, width = near_ref.shape
    length = points // blocks
    half = points // 2
    order_n = width + length
    rim_start = points - RIM

    def region_peer(i):
        return lax.rem(reg + i, n_reg)

    def band_peer(i):
        return lax.rem(band + i, n_band)

    arrivals = [
        pltpu.make_async_copy(source, target, local_sems.at[k])
        for k, (source, target) in enumerate(
            [(coords_hbm, coords_ref), (near_hbm, near_ref), (values_hbm, values_ref), (params_hbm, params_ref)]
        )
    ]
    for copy in arrivals:
        copy.start()

    barrier = pltpu.get_barrier_semaphore()

    def greet_region(i, c):
        pl.semaphore_signal(barrier, inc=1, device_id=(band, region_peer(i)), device_id_type=MESH)
        return c

    for i in (1, n_band - 1):
        pl.semaphore_signal(barrier, inc=1, device_id=(band_peer(i), reg), device_id_type=MESH)
    lax.fori_loop(1, n_reg, greet_region, 0)

    rounds = []
    while 2 ** (len(rounds) + 1) <= n_band // 2:
        rounds.append(2 ** len(rounds))

    def tell(k):
        for side, by in enumerate((rounds[k], n_band - rounds[k])):
            pl.semaphore_signal(
                known_sems.at[k, side], inc=1, device_id=(band_peer(by), reg), device_id_type=MESH
            )

    def hear(k):
        for side in range(2):
            pl.semaphore_wait(known_sems.at[k, side], 1)

    def to_peers(source, into, stage):
        def send(i, c):
            peer = region_peer(i)
            pltpu.make_async_remote_copy(
                src_ref=source(peer), dst_ref=into.at[reg],
                send_sem=send_sems.at[stage], recv_sem=recv_sems.at[stage],
                device_id=(band, peer), device_id_type=MESH,
            ).start()
            return c
        lax.fori_loop(1, n_reg, send, 0)

    def from_peers(into, stage):
        some = pl.ds(0, n_reg - 1)
        return pltpu.make_async_remote_copy(
            src_ref=into.at[some], dst_ref=into.at[some],
            send_sem=send_sems.at[stage], recv_sem=recv_sems.at[stage],
            device_id=(band, region_peer(1)), device_id_type=MESH,
        )

    def up_band(source, into, stage, by):
        return pltpu.make_async_remote_copy(
            src_ref=source, dst_ref=into, send_sem=send_sems.at[stage], recv_sem=recv_sems.at[stage],
            device_id=(band_peer(by), reg), device_id_type=MESH,
        )

    arrivals[0].wait()
    pl.semaphore_wait(barrier, n_reg + 1)
    to_peers(lambda peer: coords_ref, place_in, 0)
    rimplace_copy = up_band(coords_ref.at[:, pl.ds(half, half)], rimplace_in, 7, 1)
    rimplace_copy.start()
    if rounds:
        tell(0)
    place_in[pl.ds(reg, 1)] = coords_ref[...][None]

    arrivals[1].wait()
    near = near_ref[...]
    owner = near // points
    offset = near - owner * points
    owner_band = owner // n_reg
    owner_reg = owner - owner_band * n_reg
    is_rim = owner_band == band - 1
    is_own = jnp.logical_and(owner_band == band, owner_reg == reg)
    is_far = jnp.logical_and(owner_band == band, owner_reg != reg)
    far_row = jnp.where(is_far, owner_reg, -1)
    table_row = jnp.where(is_rim, n_reg, owner_reg)
    off_t = [(iota((points, width), 0) == offset[b : b + 1]).astype(BF16) for b in range(blocks)]
    far_t = [(iota((n_reg, width), 0) == far_row[b : b + 1]).astype(F32) for b in range(blocks)]
    counts = sum(nt(far_t[b].astype(BF16), off_t[b]) for b in range(blocks))
    mask = (counts > 0.5).astype(F32)
    below = (iota((points, points), 0) < iota((points, points), 1)).astype(BF16)
    rank = nn(mask.astype(BF16), below)
    ask_out[:, 0, :] = mask[:, :half]
    ask_out[:, 1, :] = mask[:, half:]
    to_peers(lambda peer: ask_out.at[peer], ask_in, 1)
    arrivals[2].wait()
    rim_copy = up_band(values_ref.at[pl.ds(rim_start, RIM)], rim_in, 4, 1)
    rim_copy.start()
    ask_in[pl.ds(reg, 1)] = jnp.zeros((1, 2, half), F32)
    rows_in[pl.ds(reg, 1)] = jnp.zeros((1, slots, reps), F32)
    back_in[pl.ds(reg, 1)] = jnp.zeros((1, slots, reps), F32)

    rank_bf = rank.astype(BF16)
    index_rows = []
    for b in range(blocks):
        slot = jnp.sum(far_t[b] * nn(rank_bf, off_t[b]), axis=0, keepdims=True).astype(jnp.int32)
        far_index = points + RIM + owner_reg[b : b + 1] * slots + slot
        rim_index = points + offset[b : b + 1] - rim_start
        index_rows.append(
            jnp.where(is_own[b : b + 1], offset[b : b + 1], jnp.where(is_rim[b : b + 1], rim_index, far_index))
        )
    table = chosen_ref.shape[2]
    index_cols = jnp.concatenate(index_rows + [jnp.zeros((8 - blocks, width), jnp.int32)], axis=0).astype(F32).T
    for b in range(blocks):
        column = index_cols[:, b : b + 1].astype(jnp.int32)
        chosen_ref[b] = (iota((width, table), 1) == column).astype(BF16)
        spread_ref[b] = (iota((table, width), 0) == index_rows[b]).astype(BF16)

    arrivals[3].wait()
    from_peers(place_in, 0).wait_recv()
    rimplace_copy.wait_recv()
    if len(rounds) > 1:
        hear(0)
        tell(1)

    x_row, y_row = coords_ref[0:1, :], coords_ref[1:2, :]
    zero_half = jnp.zeros((1, half), F32)
    tables = []
    for k in range(2):
        rim_row = jnp.concatenate([zero_half, rimplace_in[k : k + 1, :]], axis=1)
        tables += [place_in[:, k, :], rim_row, jnp.zeros((7, points), F32)]
    coord_table = jnp.concatenate(tables, axis=0)
    rows = n_reg + 8
    variance = jnp.exp(jnp.full((1, 1), params_ref[0], F32))
    inverse_range = jnp.sqrt(jnp.full((1, 1), 3.0, F32)) * jnp.exp(jnp.full((1, 1), -params_ref[1], F32))
    nugget = jnp.exp(jnp.full((1, 1), params_ref[2], F32))
    parts = split(coord_table, 3)
    for b in range(blocks):
        own_t = (iota((rows, width), 0) == table_row[b : b + 1]).astype(F32)
        found = sum(nn(part, off_t[b]) for part in reversed(parts))
        x_near = jnp.sum(own_t * found[:rows], axis=0, keepdims=True)
        y_near = jnp.sum(own_t * found[rows:], axis=0, keepdims=True)
        here = slice(b * length, (b + 1) * length)
        x_joint = jnp.concatenate([x_near, x_row[:, here]], axis=1)
        y_joint = jnp.concatenate([y_near, y_row[:, here]], axis=1)
        cols = jnp.concatenate([x_joint, y_joint, jnp.zeros((6, order_n), F32)], axis=0).T
        delta_x = cols[:, 0:1] - x_joint
        delta_y = cols[:, 1:2] - y_joint
        scaled = inverse_range * jnp.sqrt(delta_x * delta_x + delta_y * delta_y)
        decayed = variance * jnp.exp(-scaled)
        shape_part = decayed + scaled * decayed
        shape_ref[b] = shape_part
        slope_ref[b] = scaled * scaled * decayed
        diagonal = iota((order_n, order_n), 0) == iota((order_n, order_n), 1)
        kern_ref[b] = jnp.where(diagonal, shape_part + nugget, shape_part)

    from_peers(ask_in, 1).wait_recv()
    wanted = jnp.concatenate([ask_in[:, 0, :], ask_in[:, 1, :]], axis=1)
    wanted_rank = nn(wanted.astype(BF16), below)
    slot_of = jnp.where(wanted > 0.5, wanted_rank, -1.0)
    sel = (
        jnp.broadcast_to(slot_of[:, None, :], (n_reg, slots, points))
        == iota((n_reg, slots, points), 1).astype(F32)
    )
    sel_ref[...] = sel.astype(F32).reshape(n_reg * slots, points).astype(BF16)
    rows_out[...] = picked(nn, sel_ref[...], values_ref[...], 2).reshape(n_reg, slots, reps)
    to_peers(lambda peer: rows_out.at[peer], rows_in, 2)

    all_blocks = range(blocks)
    inv_a = inverses([kern_ref[b, :width, :width] for b in all_blocks], [inv_a0, inv_a1], nugget, 5)
    x_t = [full(kern_ref[b, width:, :width], inv_a[b]) for b in all_blocks]
    x_n = [x.T for x in x_t]
    schur = [kern_ref[b, width:, width:] - three_pass(x_t[b], kern_ref[b, :width, width:]) for b in all_blocks]
    if len(rounds) > 2:
        hear(1)
        tell(2)
    inv_s = inverses(schur, [inv_s0, inv_s1], nugget, 4)

    rim_copy.wait_recv()
    from_peers(rows_in, 2).wait_recv()
    pad = table - points - RIM - n_reg * slots
    value_table = jnp.concatenate(
        [values_ref[...], rim_in[...], rows_in[...].reshape(n_reg * slots, reps), jnp.zeros((pad, reps), F32)],
        axis=0,
    )
    value_parts = split(value_table, 2)
    near_rows = [sum(nn(chosen_ref[b], part) for part in reversed(value_parts)) for b in all_blocks]
    own_rows = [values_ref[b * length : (b + 1) * length, :] for b in all_blocks]
    resids = [own_rows[b] - three_pass(x_t[b], near_rows[b]) for b in all_blocks]
    heads = [three_pass(inv_a[b], near_rows[b]) for b in all_blocks]
    us = [three_pass(inv_s[b], resids[b]) for b in all_blocks]
    backs = [three_pass(x_n[b], us[b]) for b in all_blocks]

    sums = [jnp.zeros((1, 1), F32)] * 3
    for b in all_blocks:
        u, head_back = us[b], -backs[b]
        back = jnp.concatenate([head_back, u], axis=0)
        left = jnp.concatenate([heads[b] + 0.5 * head_back, 0.5 * u], axis=0)
        v = jnp.concatenate(
            [-x_n[b], (iota((length, length), 0) == iota((length, length), 1)).astype(F32)], axis=0
        )
        vs = (-0.5 * reps) * jnp.concatenate([-three_pass(x_n[b], inv_s[b]), inv_s[b]], axis=0)
        left = jnp.concatenate([left, vs], axis=1)
        right = jnp.concatenate([back, v], axis=1)
        grad_kernel = three_pass(left, right, nt)
        total = lambda z: jnp.sum(jnp.sum(z, axis=0, keepdims=True), axis=1, keepdims=True)
        sums = [
            sums[0] + total(grad_kernel * shape_ref[b]),
            sums[1] + total(grad_kernel * slope_ref[b]),
            sums[2] + nugget * total(left * right),
        ]
    lane = iota((1, half), 1)
    mine = jnp.where(lane == 0, sums[0], jnp.where(lane == 1, sums[1], jnp.where(lane == 2, sums[2], 0.0)))
    th_out[...] = mine
    to_peers(lambda peer: th_out, th_in, 5)
    th_in[pl.ds(reg, 1)] = mine[None]

    spread = sum(picked(nn, spread_ref[b], backs[b], 2) for b in all_blocks)
    back_out[...] = spread[points + RIM : points + RIM + n_reg * slots].reshape(n_reg, slots, reps)
    rimback_out[...] = spread[points : points + RIM]
    grad_ref[...] = spread[:points] - jnp.concatenate(us, axis=0)
    if rounds:
        hear(len(rounds) - 1)
    from_peers(th_in, 5).wait_recv()
    band_sum = jnp.sum(th_in[...], axis=0)
    tb_out[...] = band_sum

    def send_band(i, c):
        pltpu.make_async_remote_copy(
            src_ref=tb_out, dst_ref=tb_in.at[band], send_sem=send_sems.at[6], recv_sem=recv_sems.at[6],
            device_id=(band_peer(i), reg), device_id_type=MESH,
        ).start()
        return c

    lax.fori_loop(1, n_band, send_band, 0)
    tb_in[pl.ds(band, 1)] = band_sum[None]
    to_peers(lambda peer: back_out.at[peer], back_in, 3)
    rimback_copy = up_band(rimback_out, rimback_in, 8, n_band - 1)
    rimback_copy.start()

    rimback_copy.wait_recv()
    from_peers(back_in, 3).wait_recv()
    returned = back_in[...].reshape(n_reg * slots, reps)
    grad_ref[...] += picked(tn, sel_ref[...], returned, 2)
    grad_ref[rim_start:, :] += rimback_in[...]

    from_bands = pltpu.make_async_remote_copy(
        src_ref=tb_in.at[pl.ds(0, n_band - 1)], dst_ref=tb_in.at[pl.ds(0, n_band - 1)],
        send_sem=send_sems.at[6], recv_sem=recv_sems.at[6],
        device_id=(band_peer(1), reg), device_id_type=MESH,
    )
    from_bands.wait_recv()
    theta_ref[...] = jnp.sum(tb_in[...], axis=0) * (1.0 / (points * n_band * n_reg * reps))

    from_peers(place_in, 0).wait_send()
    from_peers(ask_in, 1).wait_send()
    from_peers(rows_in, 2).wait_send()
    from_peers(back_in, 3).wait_send()
    from_peers(th_in, 5).wait_send()
    from_bands.wait_send()
    rimplace_copy.wait_send()
    rim_copy.wait_send()
    rimback_copy.wait_send()


def shards(n_band, n_reg, values, coords, neighbours, log_params):
    points, reps = values.shape
    blocks, width = neighbours.shape
    length = points // blocks
    order_n = width + length
    cap = (2 * POOL + n_reg - 2) // (n_reg - 1)
    slots = -(-cap // 16) * 16
    table = -(-(points + RIM + n_reg * slots) // 128) * 128
    half = points // 2
    vmem = lambda *shape: pltpu.VMEM(shape, F32)
    grad, theta = pl.pallas_call(
        functools.partial(kernel, n_band, n_reg, slots),
        out_shape=(jax.ShapeDtypeStruct((points, reps), F32), jax.ShapeDtypeStruct((1, half), F32)),
        in_specs=[pl.BlockSpec(memory_space=pltpu.HBM)] * 4,
        out_specs=(pl.BlockSpec(memory_space=pltpu.VMEM), pl.BlockSpec(memory_space=pltpu.VMEM)),
        scratch_shapes=[
            vmem(points, reps), vmem(2, points), pltpu.VMEM((blocks, width), jnp.int32),
            pltpu.SMEM((3,), F32),
            vmem(n_reg, 2, points),
            vmem(n_reg, 2, half), vmem(n_reg, 2, half),
            vmem(n_reg, slots, reps), vmem(n_reg, slots, reps),
            vmem(n_reg, slots, reps), vmem(n_reg, slots, reps),
            vmem(2, half), vmem(RIM, reps), vmem(RIM, reps), vmem(RIM, reps),
            vmem(1, half), vmem(n_reg, 1, half), vmem(1, half), vmem(n_band, 1, half),
            pltpu.VMEM((blocks, width, table), BF16), pltpu.VMEM((blocks, table, width), BF16),
            pltpu.VMEM((n_reg * slots, points), BF16),
            vmem(blocks, order_n, order_n), vmem(blocks, order_n, order_n), vmem(blocks, order_n, order_n),
            vmem(2 * width, width), vmem(2 * width, width), vmem(2 * length, length), vmem(2 * length, length),
            pltpu.SemaphoreType.DMA((4,)), pltpu.SemaphoreType.DMA((9,)), pltpu.SemaphoreType.DMA((9,)),
            pltpu.SemaphoreType.REGULAR((4, 2)),
        ],
        compiler_params=pltpu.CompilerParams(
            collective_id=0, has_side_effects=True, vmem_limit_bytes=60 * 1024 * 1024
        ),
    )(values, coords, neighbours, log_params)
    return grad, theta[0, :3]


def solution(mesh):
    placed = (
        P(("band", "region"), None),
        P(None, ("band", "region")),
        P(("band", "region"), None),
        P(),
    )
    return jax.shard_map(
        functools.partial(shards, mesh.shape["band"], mesh.shape["region"]),
        mesh=mesh,
        in_specs=placed,
        out_specs=(P(("band", "region"), None), P()),
        check_vma=False,
    )
```

time: 55.7 us -> 49 us (0.88)
  Pallas kernels: 50.8 us -> 45.5 us
  local copies, waits for them, and re-layouts: 4.08 us -> 2.72 us
    pallas_call x1, Pallas kernels: 50.8 us -> 45.5 us  [shards(): pl.pallas_call(functools.partial(kernel, n_band, n_reg, slots), out_shape...]
    unnamed x9 -> x3, local copies, waits for them, and re-layouts: 3.57 us -> 2.21 us
where the time goes in v2:
time: 49 us; the launch traced here: 48.9 us
  Pallas kernels  45.5 us (93%)
  local copies, waits for them, and re-layouts  2.72 us (6%)
  between operations  0.65 us (1%)
    pallas_call x1, Pallas kernels, shards(): pl.pallas_call(functools.partial(kernel, n_band, n_reg, slots), out_shape...  45.5 us
    unnamed x3, local copies, waits for them, and re-layouts  2.21 us

profile of v2, /device:TPU:1, one launch (start us, length us, event | category | flops | bytes accessed | tf_op | source)
XLA Modules:
  0.0 48.9 jit_solution(12731493269193198384)
XLA Ops:
  0.6 45.5 %shard_map.59 = (f32[256,128]{1,0:T(8,128)}, f32[1,128]{1,0:T(1,128)}) custom-call(f32[256,128]{1,0:T(8,128)} %values_hbm.1, f32[2,256]{1,0:T(2,128)} %coords_hbm.1, s32[2,256]{1,0:T(2,128)} %near_hbm.1, f32[3]{0:T(128)} %params_hbm.1), custom_call_target="tpu_custom_call" | custom-call | tf_op jit(solution)/shard_map/pallas_call | solution.py:396
  46.1 0.0 copy-start
  46.1 0.6 %copy-done = f32[1,128]{1,0:T(1,128)S(1)} copy-done((f32[1,128]{1,0:T(1,128)S(1)}, f32[1,128]{1,0:T(1,128)}, u32[]{:S(2)}) %copy-start) | copy-done | bytes 536
  46.8 0.5 %slice_bitcast_fusion = f32[3]{0:T(128)} fusion(f32[1,128]{1,0:T(1,128)S(1)} %copy-done), kind=kLoop, calls=%fused_computation | loop fusion | bytes 24 | tf_op jit(solution)/shard_map/squeeze | solution.py:421
  47.3 1.6 %copy.7 = f32[256,128]{1,0:T(8,128)} copy(f32[256,128]{1,0:T(8,128)} %get-tuple-element.8) | data formatting | bytes 262144
Async XLA Ops:
  46.1 0.7 %copy-start = (f32[1,128]{1,0:T(1,128)S(1)}, f32[1,128]{1,0:T(1,128)}, u32[]{:S(2)}) copy-start(f32[1,128]{1,0:T(1,128)} %get-tuple-element.5) | copy-start | bytes 1540

commit v3 on v2

--- a/solution.py
+++ b/solution.py
@@ -43,10 +43,6 @@
     return dot(a_high, b_high) + (dot(a_high, b_low) + dot(a_low, b_high))
 
 
-def full(a, b):
-    return jnp.dot(a, b, precision=lax.Precision.HIGHEST, preferred_element_type=F32)
-
-
 def picked(dot, chosen, x, parts):
     return sum(dot(chosen, part) for part in reversed(split(x, parts)))
 
@@ -55,7 +51,7 @@
     return lax.broadcasted_iota(jnp.int32, shape, dim)
 
 
-def inverses(mats, refs, lowest, carried):
+def inverses(mats, refs, lowest, carried, last):
     n = mats[0].shape[0]
     eye = (iota((n, n), 0) == iota((n, n), 1)).astype(F32)
 
@@ -94,8 +90,10 @@
     found = [ref[:n] for ref in refs]
     products = [three_pass(mat, x) for mat, x in zip(mats, found)]
     found = [three_pass(x, factor_of(product, low)) for x, product, low in zip(found, products, lows)]
+    if not last:
+        return found
     lows = [raised(low) for low in lows]
-    products = [full(mat, x) for mat, x in zip(mats, found)]
+    products = [three_pass(mat, x) for mat, x in zip(mats, found)]
     return [
         x + three_pass(x, factor_of(product, low) - eye) for x, product, low in zip(found, products, lows)
     ]
@@ -120,8 +118,22 @@
     order_n = width + length
     rim_start = points - RIM
 
+    def turned(k, n):
+        by = (k + 1) // 2
+        return lax.rem(n // 2 + jnp.where(lax.rem(k, 2) == 0, by, n - by), n)
+
+    side = 1
+    while 2 * (2 * side) ** 2 <= n_reg:
+        side *= 2
+    tall = n_reg // (2 * side)
+
     def region_peer(i):
-        return lax.rem(reg + i, n_reg)
+        k = i - 1
+        y, x, core = reg // (2 * side), lax.rem(reg // 2, side), lax.rem(reg, 2)
+        y = lax.rem(y + turned(k // (2 * side), tall), tall)
+        x = lax.rem(x + turned(lax.rem(k // 2, side), side), side)
+        core = lax.rem(core + 1 + lax.rem(k, 2), 2)
+        return (y * side + x) * 2 + core
 
     def band_peer(i):
         return lax.rem(band + i, n_band)
@@ -287,14 +299,16 @@
     to_peers(lambda peer: rows_out.at[peer], rows_in, 2)
 
     all_blocks = range(blocks)
-    inv_a = inverses([kern_ref[b, :width, :width] for b in all_blocks], [inv_a0, inv_a1], nugget, 5)
-    x_t = [full(kern_ref[b, width:, :width], inv_a[b]) for b in all_blocks]
+    inv_a = inverses([kern_ref[b, :width, :width] for b in all_blocks], [inv_a0, inv_a1], nugget, 5, False)
+    x_t = [three_pass(kern_ref[b, width:, :width], inv_a[b]) for b in all_blocks]
+    missed = [kern_ref[b, width:, :width] - three_pass(x_t[b], kern_ref[b, :width, :width]) for b in all_blocks]
+    x_t = [x_t[b] + three_pass(missed[b], inv_a[b]) for b in all_blocks]
     x_n = [x.T for x in x_t]
     schur = [kern_ref[b, width:, width:] - three_pass(x_t[b], kern_ref[b, :width, width:]) for b in all_blocks]
     if len(rounds) > 2:
         hear(1)
         tell(2)
-    inv_s = inverses(schur, [inv_s0, inv_s1], nugget, 4)
+    inv_s = inverses(schur, [inv_s0, inv_s1], nugget, 4, True)
 
     rim_copy.wait_recv()
     from_peers(rows_in, 2).wait_recv()
@@ -308,6 +322,8 @@
     own_rows = [values_ref[b * length : (b + 1) * length, :] for b in all_blocks]
     resids = [own_rows[b] - three_pass(x_t[b], near_rows[b]) for b in all_blocks]
     heads = [three_pass(inv_a[b], near_rows[b]) for b in all_blocks]
+    missed = [near_rows[b] - three_pass(kern_ref[b, :width, :width], heads[b]) for b in all_blocks]
+    heads = [heads[b] + three_pass(inv_a[b], missed[b]) for b in all_blocks]
     us = [three_pass(inv_s[b], resids[b]) for b in all_blocks]
     backs = [three_pass(x_n[b], us[b]) for b in all_blocks]
 
@@ -352,7 +368,7 @@
         ).start()
         return c
 
-    lax.fori_loop(1, n_band, send_band, 0)
+    lax.fori_loop(0, n_band - 1, lambda k, c: send_band(turned(k, n_band), c), 0)
     tb_in[pl.ds(band, 1)] = band_sum[None]
     to_peers(lambda peer: back_out.at[peer], back_in, 3)
     rimback_copy = up_band(rimback_out, rimback_in, 8, n_band - 1)
@@ -395,7 +411,7 @@
     vmem = lambda *shape: pltpu.VMEM(shape, F32)
     grad, theta = pl.pallas_call(
         functools.partial(kernel, n_band, n_reg, slots),
-        out_shape=(jax.ShapeDtypeStruct((points, reps), F32), jax.ShapeDtypeStruct((1, half), F32)),
+        out_shape=(pltpu.VMEM((points, reps), F32), pltpu.VMEM((1, half), F32)),
         in_specs=[pl.BlockSpec(memory_space=pltpu.HBM)] * 4,
         out_specs=(pl.BlockSpec(memory_space=pltpu.VMEM), pl.BlockSpec(memory_space=pltpu.VMEM)),
         scratch_shapes=[

time: 49 us -> 47.4 us (0.967)
  local copies, waits for them, and re-layouts: 2.72 us -> 1.17 us
    unnamed x3 -> x1, local copies, waits for them, and re-layouts: 2.21 us -> 0.66 us
where the time goes in v3:
time: 47.4 us; the launch traced here: 47.3 us
  Pallas kernels  45.5 us (96%)
  local copies, waits for them, and re-layouts  1.17 us (2%)
  between operations  0.64 us (1%)
    pallas_call x1, Pallas kernels, shards(): pl.pallas_call(functools.partial(kernel, n_band, n_reg, slots), out_shape...  45.5 us

profile of v3, /device:TPU:1, one launch (start us, length us, event | category | flops | bytes accessed | tf_op | source)
XLA Modules:
  0.0 47.3 jit_solution(2436139654246512495)
XLA Ops:
  0.6 45.5 %shard_map.59 = (f32[256,128]{1,0:T(8,128)S(1)}, f32[1,128]{1,0:T(1,128)S(1)}) custom-call(f32[256,128]{1,0:T(8,128)} %values_hbm.1, f32[2,256]{1,0:T(2,128)} %coords_hbm.1, s32[2,256]{1,0:T(2,128)} %near_hbm.1, f32[3]{0:T(128)} %params_hbm.1), custom_call_target="tpu_custom_call" | custom-call | tf_op jit(solution)/shard_map/pallas_call | solution.py:412
  46.1 0.7 %copy.7 = f32[256,128]{1,0:T(8,128)} copy(f32[256,128]{1,0:T(8,128)S(1)} %get-tuple-element.6) | data formatting | bytes 262144
  46.8 0.5 %slice_bitcast_fusion = f32[3]{0:T(128)} fusion(f32[1,128]{1,0:T(1,128)S(1)} %get-tuple-element.5), kind=kLoop, calls=%fused_computation | loop fusion | bytes 24 | tf_op jit(solution)/shard_map/squeeze | solution.py:437

commit v4 on v3

--- a/solution.py
+++ b/solution.py
@@ -40,11 +40,21 @@
 def three_pass(a, b, dot=nn):
     a_high, a_low = split(a, 2)
     b_high, b_low = split(b, 2)
+    n = b.shape[1]
+    if dot is nn and n <= 128:
+        wide = jnp.concatenate([b_high, b_low], axis=1)
+        if a.shape[1] <= 128:
+            both = nn(jnp.concatenate([a_high, a_low], axis=1), jnp.concatenate([wide, wide], axis=0))
+            return both[:, :n] + both[:, n:]
+        both = nn(a_high, wide)
+        return both[:, :n] + (both[:, n:] + nn(a_low, b_high))
     return dot(a_high, b_high) + (dot(a_high, b_low) + dot(a_low, b_high))
 
 
-def picked(dot, chosen, x, parts):
-    return sum(dot(chosen, part) for part in reversed(split(x, parts)))
+def picked(dot, chosen, x):
+    n = x.shape[1]
+    both = dot(chosen, jnp.concatenate(split(x, 2), axis=1))
+    return both[:, :n] + both[:, n:]
 
 
 def iota(shape, dim):
@@ -62,7 +72,7 @@
     def raised(low):
         return 4.0 * low / ((1.0 + low) * (1.0 + low))
 
-    lows, factors, starts = [], [], []
+    lows, overs, factors, starts = [], [], [], []
     for mat in mats:
         sums = jnp.sum(jnp.abs(mat), axis=0, keepdims=True)
         over = 1.0 / (jnp.max(sums, axis=1, keepdims=True) * 1.0001)
@@ -70,24 +80,16 @@
         start = over * mat
         factor = factor_of(start, low)
         starts.append(start)
+        overs.append(over)
         factors.append(factor)
         lows.append(raised(low))
     products = [three_pass(start, factor) for start, factor in zip(starts, factors)]
-    for mat, ref, factor, product in zip(mats, refs, factors, products):
-        over = jnp.max(jnp.sum(jnp.abs(mat), axis=0, keepdims=True), axis=1, keepdims=True) * 1.0001
-        ref[:n] = factor / over
-        ref[n:] = product
-
-    def step(i, lows):
-        held = [ref[...] for ref in refs]
-        factors = [factor_of(both[n:], low) for both, low in zip(held, lows)]
-        both = [three_pass(x, factor) for x, factor in zip(held, factors)]
-        for ref, x in zip(refs, both):
-            ref[...] = x
-        return tuple(raised(low) for low in lows)
-
-    lows = lax.fori_loop(0, carried, step, tuple(lows))
-    found = [ref[:n] for ref in refs]
+    found = [over * factor for over, factor in zip(overs, factors)]
+    for _ in range(carried):
+        factors = [factor_of(product, low) for product, low in zip(products, lows)]
+        found = [three_pass(x, factor) for x, factor in zip(found, factors)]
+        products = [three_pass(product, factor) for product, factor in zip(products, factors)]
+        lows = [raised(low) for low in lows]
     products = [three_pass(mat, x) for mat, x in zip(mats, found)]
     found = [three_pass(x, factor_of(product, low)) for x, product, low in zip(found, products, lows)]
     if not last:
@@ -198,9 +200,9 @@
 
     arrivals[0].wait()
     pl.semaphore_wait(barrier, n_reg + 1)
-    to_peers(lambda peer: coords_ref, place_in, 0)
     rimplace_copy = up_band(coords_ref.at[:, pl.ds(half, half)], rimplace_in, 7, 1)
     rimplace_copy.start()
+    to_peers(lambda peer: coords_ref, place_in, 0)
     if rounds:
         tell(0)
     place_in[pl.ds(reg, 1)] = coords_ref[...][None]
@@ -251,9 +253,6 @@
     arrivals[3].wait()
     from_peers(place_in, 0).wait_recv()
     rimplace_copy.wait_recv()
-    if len(rounds) > 1:
-        hear(0)
-        tell(1)
 
     x_row, y_row = coords_ref[0:1, :], coords_ref[1:2, :]
     zero_half = jnp.zeros((1, half), F32)
@@ -295,7 +294,7 @@
         == iota((n_reg, slots, points), 1).astype(F32)
     )
     sel_ref[...] = sel.astype(F32).reshape(n_reg * slots, points).astype(BF16)
-    rows_out[...] = picked(nn, sel_ref[...], values_ref[...], 2).reshape(n_reg, slots, reps)
+    rows_out[...] = picked(nn, sel_ref[...], values_ref[...]).reshape(n_reg, slots, reps)
     to_peers(lambda peer: rows_out.at[peer], rows_in, 2)
 
     all_blocks = range(blocks)
@@ -305,11 +304,14 @@
     x_t = [x_t[b] + three_pass(missed[b], inv_a[b]) for b in all_blocks]
     x_n = [x.T for x in x_t]
     schur = [kern_ref[b, width:, width:] - three_pass(x_t[b], kern_ref[b, :width, width:]) for b in all_blocks]
+    if len(rounds) > 1:
+        hear(0)
+        tell(1)
+    inv_s = inverses(schur, [inv_s0, inv_s1], nugget, 4, True)
+
     if len(rounds) > 2:
         hear(1)
         tell(2)
-    inv_s = inverses(schur, [inv_s0, inv_s1], nugget, 4, True)
-
     rim_copy.wait_recv()
     from_peers(rows_in, 2).wait_recv()
     pad = table - points - RIM - n_reg * slots
@@ -317,8 +319,7 @@
         [values_ref[...], rim_in[...], rows_in[...].reshape(n_reg * slots, reps), jnp.zeros((pad, reps), F32)],
         axis=0,
     )
-    value_parts = split(value_table, 2)
-    near_rows = [sum(nn(chosen_ref[b], part) for part in reversed(value_parts)) for b in all_blocks]
+    near_rows = [picked(nn, chosen_ref[b], value_table) for b in all_blocks]
     own_rows = [values_ref[b * length : (b + 1) * length, :] for b in all_blocks]
     resids = [own_rows[b] - three_pass(x_t[b], near_rows[b]) for b in all_blocks]
     heads = [three_pass(inv_a[b], near_rows[b]) for b in all_blocks]
@@ -351,7 +352,7 @@
     to_peers(lambda peer: th_out, th_in, 5)
     th_in[pl.ds(reg, 1)] = mine[None]
 
-    spread = sum(picked(nn, spread_ref[b], backs[b], 2) for b in all_blocks)
+    spread = sum(picked(nn, spread_ref[b], backs[b]) for b in all_blocks)
     back_out[...] = spread[points + RIM : points + RIM + n_reg * slots].reshape(n_reg, slots, reps)
     rimback_out[...] = spread[points : points + RIM]
     grad_ref[...] = spread[:points] - jnp.concatenate(us, axis=0)
@@ -377,7 +378,7 @@
     rimback_copy.wait_recv()
     from_peers(back_in, 3).wait_recv()
     returned = back_in[...].reshape(n_reg * slots, reps)
-    grad_ref[...] += picked(tn, sel_ref[...], returned, 2)
+    grad_ref[...] += picked(tn, sel_ref[...], returned)
     grad_ref[rim_start:, :] += rimback_in[...]
 
     from_bands = pltpu.make_async_remote_copy(

time: 47.4 us -> 46 us (0.970)
  Pallas kernels: 45.5 us -> 44.1 us
    pallas_call x1, Pallas kernels: 45.5 us -> 44.1 us  [shards(): pl.pallas_call(functools.partial(kernel, n_band, n_reg, slots), out_shape...]
where the time goes in v4:
time: 46 us; the launch traced here: 45.9 us
  Pallas kernels  44.1 us (96%)
  local copies, waits for them, and re-layouts  1.17 us (3%)
  between operations  0.64 us (1%)
    pallas_call x1, Pallas kernels, shards(): pl.pallas_call(functools.partial(kernel, n_band, n_reg, slots), out_shape...  44.1 us

profile of v4, /device:TPU:1, one launch (start us, length us, event | category | flops | bytes accessed | tf_op | source)
XLA Modules:
  0.0 45.9 jit_solution(9636523028461338199)
XLA Ops:
  0.6 44.1 %shard_map.59 = (f32[256,128]{1,0:T(8,128)S(1)}, f32[1,128]{1,0:T(1,128)S(1)}) custom-call(f32[256,128]{1,0:T(8,128)} %values_hbm.1, f32[2,256]{1,0:T(2,128)} %coords_hbm.1, s32[2,256]{1,0:T(2,128)} %near_hbm.1, f32[3]{0:T(128)} %params_hbm.1), custom_call_target="tpu_custom_call" | custom-call | tf_op jit(solution)/shard_map/pallas_call | solution.py:413
  44.7 0.7 %copy.7 = f32[256,128]{1,0:T(8,128)} copy(f32[256,128]{1,0:T(8,128)S(1)} %get-tuple-element.6) | data formatting | bytes 262144
  45.4 0.5 %slice_bitcast_fusion = f32[3]{0:T(128)} fusion(f32[1,128]{1,0:T(1,128)S(1)} %get-tuple-element.5), kind=kLoop, calls=%fused_computation | loop fusion | bytes 24 | tf_op jit(solution)/shard_map/squeeze | solution.py:438

commit v5 on v4

--- a/solution.py
+++ b/solution.py
@@ -61,7 +61,7 @@
     return lax.broadcasted_iota(jnp.int32, shape, dim)
 
 
-def inverses(mats, refs, lowest, carried, last):
+def inverses(mats, lowest, carried, last):
     n = mats[0].shape[0]
     eye = (iota((n, n), 0) == iota((n, n), 1)).astype(F32)
 
@@ -109,7 +109,7 @@
     place_in, ask_out, ask_in, rows_out, rows_in, back_out, back_in,
     rimplace_in, rim_in, rimback_out, rimback_in,
     th_out, th_in, tb_out, tb_in,
-    chosen_ref, spread_ref, sel_ref, kern_ref, shape_ref, slope_ref, inv_a0, inv_a1, inv_s0, inv_s1,
+    chosen_ref, spread_ref, sel_ref, kern_ref, shape_ref, slope_ref,
     local_sems, send_sems, recv_sems, known_sems,
 ):
     band, reg = lax.axis_index("band"), lax.axis_index("region")
@@ -297,17 +297,17 @@
     rows_out[...] = picked(nn, sel_ref[...], values_ref[...]).reshape(n_reg, slots, reps)
     to_peers(lambda peer: rows_out.at[peer], rows_in, 2)
 
+    if len(rounds) > 1:
+        hear(0)
+        tell(1)
     all_blocks = range(blocks)
-    inv_a = inverses([kern_ref[b, :width, :width] for b in all_blocks], [inv_a0, inv_a1], nugget, 5, False)
+    inv_a = inverses([kern_ref[b, :width, :width] for b in all_blocks], nugget, 5, False)
     x_t = [three_pass(kern_ref[b, width:, :width], inv_a[b]) for b in all_blocks]
     missed = [kern_ref[b, width:, :width] - three_pass(x_t[b], kern_ref[b, :width, :width]) for b in all_blocks]
     x_t = [x_t[b] + three_pass(missed[b], inv_a[b]) for b in all_blocks]
     x_n = [x.T for x in x_t]
     schur = [kern_ref[b, width:, width:] - three_pass(x_t[b], kern_ref[b, :width, width:]) for b in all_blocks]
-    if len(rounds) > 1:
-        hear(0)
-        tell(1)
-    inv_s = inverses(schur, [inv_s0, inv_s1], nugget, 4, True)
+    inv_s = inverses(schur, nugget, 4, True)
 
     if len(rounds) > 2:
         hear(1)
@@ -427,7 +427,6 @@
             pltpu.VMEM((blocks, width, table), BF16), pltpu.VMEM((blocks, table, width), BF16),
             pltpu.VMEM((n_reg * slots, points), BF16),
             vmem(blocks, order_n, order_n), vmem(blocks, order_n, order_n), vmem(blocks, order_n, order_n),
-            vmem(2 * width, width), vmem(2 * width, width), vmem(2 * length, length), vmem(2 * length, length),
             pltpu.SemaphoreType.DMA((4,)), pltpu.SemaphoreType.DMA((9,)), pltpu.SemaphoreType.DMA((9,)),
             pltpu.SemaphoreType.REGULAR((4, 2)),
         ],

time: 46 us -> 45.8 us (level)
  no operation moved by 1% of the time
where the time goes in v5:
time: 45.8 us; the launch traced here: 45.7 us
  Pallas kernels  43.8 us (96%)
  local copies, waits for them, and re-layouts  1.17 us (3%)
  between operations  0.64 us (1%)
    pallas_call x1, Pallas kernels, shards(): pl.pallas_call(functools.partial(kernel, n_band, n_reg, slots), out_shape...  43.8 us

profile of v5, /device:TPU:1, one launch (start us, length us, event | category | flops | bytes accessed | tf_op | source)
XLA Modules:
  0.0 45.7 jit_solution(7962617745016972444)
XLA Ops:
  0.6 43.8 %shard_map.59 = (f32[256,128]{1,0:T(8,128)S(1)}, f32[1,128]{1,0:T(1,128)S(1)}) custom-call(f32[256,128]{1,0:T(8,128)} %values_hbm.1, f32[2,256]{1,0:T(2,128)} %coords_hbm.1, s32[2,256]{1,0:T(2,128)} %near_hbm.1, f32[3]{0:T(128)} %params_hbm.1), custom_call_target="tpu_custom_call" | custom-call | tf_op jit(solution)/shard_map/pallas_call | solution.py:413
  44.5 0.7 %copy.7 = f32[256,128]{1,0:T(8,128)} copy(f32[256,128]{1,0:T(8,128)S(1)} %get-tuple-element.6) | data formatting | bytes 262144
  45.1 0.5 %slice_bitcast_fusion = f32[3]{0:T(128)} fusion(f32[1,128]{1,0:T(1,128)S(1)} %get-tuple-element.5), kind=kLoop, calls=%fused_computation | loop fusion | bytes 24 | tf_op jit(solution)/shard_map/squeeze | solution.py:437

commit v6 on v5

--- a/solution.py
+++ b/solution.py
@@ -106,7 +106,7 @@
     values_hbm, coords_hbm, near_hbm, params_hbm,
     grad_ref, theta_ref,
     values_ref, coords_ref, near_ref, params_ref,
-    place_in, ask_out, ask_in, rows_out, rows_in, back_out, back_in,
+    ask_out, ask_in, rows_out, rows_in, back_out, back_in,
     rimplace_in, rim_in, rimback_out, rimback_in,
     th_out, th_in, tb_out, tb_in,
     chosen_ref, spread_ref, sel_ref, kern_ref, shape_ref, slope_ref,
@@ -157,7 +157,7 @@
 
     for i in (1, n_band - 1):
         pl.semaphore_signal(barrier, inc=1, device_id=(band_peer(i), reg), device_id_type=MESH)
-    lax.fori_loop(1, n_reg, greet_region, 0)
+    lax.fori_loop(1, n_reg, greet_region, 0, unroll=True)
 
     rounds = []
     while 2 ** (len(rounds) + 1) <= n_band // 2:
@@ -182,7 +182,7 @@
                 device_id=(band, peer), device_id_type=MESH,
             ).start()
             return c
-        lax.fori_loop(1, n_reg, send, 0)
+        lax.fori_loop(1, n_reg, send, 0, unroll=True)
 
     def from_peers(into, stage):
         some = pl.ds(0, n_reg - 1)
@@ -197,15 +197,6 @@
             src_ref=source, dst_ref=into, send_sem=send_sems.at[stage], recv_sem=recv_sems.at[stage],
             device_id=(band_peer(by), reg), device_id_type=MESH,
         )
-
-    arrivals[0].wait()
-    pl.semaphore_wait(barrier, n_reg + 1)
-    rimplace_copy = up_band(coords_ref.at[:, pl.ds(half, half)], rimplace_in, 7, 1)
-    rimplace_copy.start()
-    to_peers(lambda peer: coords_ref, place_in, 0)
-    if rounds:
-        tell(0)
-    place_in[pl.ds(reg, 1)] = coords_ref[...][None]
 
     arrivals[1].wait()
     near = near_ref[...]
@@ -224,13 +215,22 @@
     mask = (counts > 0.5).astype(F32)
     below = (iota((points, points), 0) < iota((points, points), 1)).astype(BF16)
     rank = nn(mask.astype(BF16), below)
-    ask_out[:, 0, :] = mask[:, :half]
-    ask_out[:, 1, :] = mask[:, half:]
+    arrivals[0].wait()
+    ask_out[:, 0, :] = jnp.broadcast_to(coords_ref[0:1, :], (n_reg, points))
+    ask_out[:, 1, :] = jnp.broadcast_to(coords_ref[1:2, :], (n_reg, points))
+    ask_out[:, 2, :] = mask
+    ask_out[:, 3, :] = jnp.zeros((n_reg, points), F32)
+
+    pl.semaphore_wait(barrier, n_reg + 1)
+    rimplace_copy = up_band(coords_ref.at[:, pl.ds(half, half)], rimplace_in, 7, 1)
+    rimplace_copy.start()
     to_peers(lambda peer: ask_out.at[peer], ask_in, 1)
+    if rounds:
+        tell(0)
     arrivals[2].wait()
     rim_copy = up_band(values_ref.at[pl.ds(rim_start, RIM)], rim_in, 4, 1)
     rim_copy.start()
-    ask_in[pl.ds(reg, 1)] = jnp.zeros((1, 2, half), F32)
+    ask_in[pl.ds(reg, 1)] = ask_out[pl.ds(reg, 1)]
     rows_in[pl.ds(reg, 1)] = jnp.zeros((1, slots, reps), F32)
     back_in[pl.ds(reg, 1)] = jnp.zeros((1, slots, reps), F32)
 
@@ -251,7 +251,7 @@
         spread_ref[b] = (iota((table, width), 0) == index_rows[b]).astype(BF16)
 
     arrivals[3].wait()
-    from_peers(place_in, 0).wait_recv()
+    from_peers(ask_in, 1).wait_recv()
     rimplace_copy.wait_recv()
 
     x_row, y_row = coords_ref[0:1, :], coords_ref[1:2, :]
@@ -259,7 +259,7 @@
     tables = []
     for k in range(2):
         rim_row = jnp.concatenate([zero_half, rimplace_in[k : k + 1, :]], axis=1)
-        tables += [place_in[:, k, :], rim_row, jnp.zeros((7, points), F32)]
+        tables += [ask_in[:, k, :], rim_row, jnp.zeros((7, points), F32)]
     coord_table = jnp.concatenate(tables, axis=0)
     rows = n_reg + 8
     variance = jnp.exp(jnp.full((1, 1), params_ref[0], F32))
@@ -285,8 +285,7 @@
         diagonal = iota((order_n, order_n), 0) == iota((order_n, order_n), 1)
         kern_ref[b] = jnp.where(diagonal, shape_part + nugget, shape_part)
 
-    from_peers(ask_in, 1).wait_recv()
-    wanted = jnp.concatenate([ask_in[:, 0, :], ask_in[:, 1, :]], axis=1)
+    wanted = ask_in[:, 2, :]
     wanted_rank = nn(wanted.astype(BF16), below)
     slot_of = jnp.where(wanted > 0.5, wanted_rank, -1.0)
     sel = (
@@ -369,7 +368,7 @@
         ).start()
         return c
 
-    lax.fori_loop(0, n_band - 1, lambda k, c: send_band(turned(k, n_band), c), 0)
+    lax.fori_loop(0, n_band - 1, lambda k, c: send_band(turned(k, n_band), c), 0, unroll=True)
     tb_in[pl.ds(band, 1)] = band_sum[None]
     to_peers(lambda peer: back_out.at[peer], back_in, 3)
     rimback_copy = up_band(rimback_out, rimback_in, 8, n_band - 1)
@@ -389,7 +388,6 @@
     from_bands.wait_recv()
     theta_ref[...] = jnp.sum(tb_in[...], axis=0) * (1.0 / (points * n_band * n_reg * reps))
 
-    from_peers(place_in, 0).wait_send()
     from_peers(ask_in, 1).wait_send()
     from_peers(rows_in, 2).wait_send()
     from_peers(back_in, 3).wait_send()
@@ -418,8 +416,7 @@
         scratch_shapes=[
             vmem(points, reps), vmem(2, points), pltpu.VMEM((blocks, width), jnp.int32),
             pltpu.SMEM((3,), F32),
-            vmem(n_reg, 2, points),
-            vmem(n_reg, 2, half), vmem(n_reg, 2, half),
+            vmem(n_reg, 4, points), vmem(n_reg, 4, points),
             vmem(n_reg, slots, reps), vmem(n_reg, slots, reps),
             vmem(n_reg, slots, reps), vmem(n_reg, slots, reps),
             vmem(2, half), vmem(RIM, reps), vmem(RIM, reps), vmem(RIM, reps),

time: 45.8 us -> 43.8 us (0.956)
  Pallas kernels: 43.8 us -> 41.8 us
    pallas_call x1, Pallas kernels: 43.8 us -> 41.8 us  [shards(): pl.pallas_call(functools.partial(kernel, n_band, n_reg, slots), out_shape...]
where the time goes in v6:
time: 43.8 us; the launch traced here: 43.6 us
  Pallas kernels  41.8 us (95%)
  local copies, waits for them, and re-layouts  1.17 us (3%)
  between operations  0.64 us (1%)
    pallas_call x1, Pallas kernels, shards(): pl.pallas_call(functools.partial(kernel, n_band, n_reg, slots), out_shape...  41.8 us

profile of v6, /device:TPU:1, one launch (start us, length us, event | category | flops | bytes accessed | tf_op | source)
XLA Modules:
  0.0 43.6 jit_solution(12356468350331186908)
XLA Ops:
  0.6 41.8 %shard_map.59 = (f32[256,128]{1,0:T(8,128)S(1)}, f32[1,128]{1,0:T(1,128)S(1)}) custom-call(f32[256,128]{1,0:T(8,128)} %values_hbm.1, f32[2,256]{1,0:T(2,128)} %coords_hbm.1, s32[2,256]{1,0:T(2,128)} %near_hbm.1, f32[3]{0:T(128)} %params_hbm.1), custom_call_target="tpu_custom_call" | custom-call | tf_op jit(solution)/shard_map/pallas_call | solution.py:411
  42.5 0.7 %copy.7 = f32[256,128]{1,0:T(8,128)} copy(f32[256,128]{1,0:T(8,128)S(1)} %get-tuple-element.6) | data formatting | bytes 262144
  43.1 0.5 %slice_bitcast_fusion = f32[3]{0:T(128)} fusion(f32[1,128]{1,0:T(1,128)S(1)} %get-tuple-element.5), kind=kLoop, calls=%fused_computation | loop fusion | bytes 24 | tf_op jit(solution)/shard_map/squeeze | solution.py:434

commit v7 on v6

--- a/solution.py
+++ b/solution.py
@@ -219,7 +219,6 @@
     ask_out[:, 0, :] = jnp.broadcast_to(coords_ref[0:1, :], (n_reg, points))
     ask_out[:, 1, :] = jnp.broadcast_to(coords_ref[1:2, :], (n_reg, points))
     ask_out[:, 2, :] = mask
-    ask_out[:, 3, :] = jnp.zeros((n_reg, points), F32)
 
     pl.semaphore_wait(barrier, n_reg + 1)
     rimplace_copy = up_band(coords_ref.at[:, pl.ds(half, half)], rimplace_in, 7, 1)
@@ -308,6 +307,12 @@
     schur = [kern_ref[b, width:, width:] - three_pass(x_t[b], kern_ref[b, :width, width:]) for b in all_blocks]
     inv_s = inverses(schur, nugget, 4, True)
 
+    one = (iota((length, length), 0) == iota((length, length), 1)).astype(F32)
+    v = [jnp.concatenate([-x_n[b], one], axis=0) for b in all_blocks]
+    vs = [
+        (-0.5 * reps) * jnp.concatenate([-three_pass(x_n[b], inv_s[b]), inv_s[b]], axis=0) for b in all_blocks
+    ]
+
     if len(rounds) > 2:
         hear(1)
         tell(2)
@@ -332,12 +337,8 @@
         u, head_back = us[b], -backs[b]
         back = jnp.concatenate([head_back, u], axis=0)
         left = jnp.concatenate([heads[b] + 0.5 * head_back, 0.5 * u], axis=0)
-        v = jnp.concatenate(
-            [-x_n[b], (iota((length, length), 0) == iota((length, length), 1)).astype(F32)], axis=0
-        )
-        vs = (-0.5 * reps) * jnp.concatenate([-three_pass(x_n[b], inv_s[b]), inv_s[b]], axis=0)
-        left = jnp.concatenate([left, vs], axis=1)
-        right = jnp.concatenate([back, v], axis=1)
+        left = jnp.concatenate([left, vs[b]], axis=1)
+        right = jnp.concatenate([back, v[b]], axis=1)
         grad_kernel = three_pass(left, right, nt)
         total = lambda z: jnp.sum(jnp.sum(z, axis=0, keepdims=True), axis=1, keepdims=True)
         sums = [
@@ -416,7 +417,7 @@
         scratch_shapes=[
             vmem(points, reps), vmem(2, points), pltpu.VMEM((blocks, width), jnp.int32),
             pltpu.SMEM((3,), F32),
-            vmem(n_reg, 4, points), vmem(n_reg, 4, points),
+            vmem(n_reg, 3, points), vmem(n_reg, 3, points),
             vmem(n_reg, slots, reps), vmem(n_reg, slots, reps),
             vmem(n_reg, slots, reps), vmem(n_reg, slots, reps),
             vmem(2, half), vmem(RIM, reps), vmem(RIM, reps), vmem(RIM, reps),

time: 43.8 us -> 43.8 us (level)
  no operation moved by 1% of the time
where the time goes in v7:
time: 43.8 us; the launch traced here: 43.6 us
  Pallas kernels  41.8 us (95%)
  local copies, waits for them, and re-layouts  1.17 us (3%)
  between operations  0.64 us (1%)
    pallas_call x1, Pallas kernels, shards(): pl.pallas_call(functools.partial(kernel, n_band, n_reg, slots), out_shape...  41.8 us

profile of v7, /device:TPU:1, one launch (start us, length us, event | category | flops | bytes accessed | tf_op | source)
XLA Modules:
  0.0 43.6 jit_solution(14407363321022336168)
XLA Ops:
  0.6 41.8 %shard_map.59 = (f32[256,128]{1,0:T(8,128)S(1)}, f32[1,128]{1,0:T(1,128)S(1)}) custom-call(f32[256,128]{1,0:T(8,128)} %values_hbm.1, f32[2,256]{1,0:T(2,128)} %coords_hbm.1, s32[2,256]{1,0:T(2,128)} %near_hbm.1, f32[3]{0:T(128)} %params_hbm.1), custom_call_target="tpu_custom_call" | custom-call | tf_op jit(solution)/shard_map/pallas_call | solution.py:412
  42.5 0.7 %copy.7 = f32[256,128]{1,0:T(8,128)} copy(f32[256,128]{1,0:T(8,128)S(1)} %get-tuple-element.6) | data formatting | bytes 262144
  43.1 0.5 %slice_bitcast_fusion = f32[3]{0:T(128)} fusion(f32[1,128]{1,0:T(1,128)S(1)} %get-tuple-element.5), kind=kLoop, calls=%fused_computation | loop fusion | bytes 24 | tf_op jit(solution)/shard_map/squeeze | solution.py:435
